TPU v7x, 128 devices: a whole 4x4x4 slice. The times are simulated.
128 devices in a mesh: rep: 8 (over y, core), sp: 16 (over z, x).
Axes of the slice: x: 4, y: 4, z: 4, core: 2. Of those that a mesh axis runs over, the one named last changes fastest.
Arguments:
- coords: float32 [8, 8192, 3, 128], P('rep', 'sp'), may hold values from -6 to 6
- atom_weight: float32 [8192, 128], P('sp'), may hold values from 0.005 to 0.05
- centers: float32 [512, 3, 128], P('sp'), may hold values from -6 to 6
- inv_width: float32 [512, 128], P('sp'), may hold values from 0.1 to 0.5
- density: float32 [512, 128], P('sp'), may hold values from 0 to 4
- variance: float32 [512, 128], P('sp'), may hold values from 1 to 4
- tile_blocks: int32 [512, 32], P('sp'), may hold values from 0 to 767, as said below
- tile_counts: int32 [512], P('sp'), may hold values from 20 to 32
- send_blocks: int32 [16, 16, 16], P('sp'), may hold values from 0 to 511, as said below
Outputs:
- forces: float32 [8, 8192, 3, 128], P('rep', 'sp')
- mean_model: float32 [512, 128], P('sp')
Inputs may be any that keep to these rules, and one draw needn't show every extreme that they name: Within one list of send_blocks the 16 block numbers differ. `tile_blocks`: within one tile's list the entries differ. Among the live entries of a device's tiles every own block is named, and every received entry 512 + s * 16 + k whose source s differs from the owner's index, cyclically, by 1 to 16 / 4 - 1 or by exactly 16 / 2; no other received entry is named anywhere.
All inputs are finite; a program needn't handle non-finite values.
Results may differ from a plain program's by a relative error of at most 0.0003.
Values sent between devices are 32-bit elements; how exact they have to be, the bound alone decides.
A program may use at most 128 MiB of HBM per device.

v0:
```python
import jax
import jax.numpy as jnp
from jax import lax
from jax.sharding import PartitionSpec as P


def gaussian_kernel(block_coords, centre, width_rate):
    offset_c = block_coords[None, :, 0, :] - centre[0][:, None, None]
    dist_sq = offset_c * offset_c
    for component in (1, 2):
        offset_c = block_coords[None, :, component, :] - centre[component][:, None, None]
        dist_sq = dist_sq + offset_c * offset_c
    return jnp.exp(-width_rate[:, None, None] * dist_sq)


def model_intersection(block_coords, block_weight, centre, width_rate):
    kernel = gaussian_kernel(block_coords, centre, width_rate)
    return jnp.einsum("gja,ja->g", kernel, block_weight, precision=lax.Precision.HIGHEST)


def restraint_pull(block_coords, block_weight, centre, width_rate, pull_rate):
    kernel = gaussian_kernel(block_coords, centre, width_rate)
    weighted = jnp.einsum("gja,g->ja", kernel, pull_rate, precision=lax.Precision.HIGHEST)
    shifted = jnp.einsum(
        "gja,cg->jca", kernel, pull_rate[None, :] * centre, precision=lax.Precision.HIGHEST
    )
    return 2.0 * block_weight[:, None, :] * (block_coords * weighted[:, None, :] - shifted)


def local(
    coords,
    atom_weight,
    centers,
    inv_width,
    density,
    variance,
    tile_blocks,
    tile_counts,
    send_blocks,
):
    sp_count = lax.axis_size("sp")
    own_coords = coords[0]
    blocks_dev = own_coords.shape[0]
    outgoing = send_blocks[0]
    per_peer = outgoing.shape[1]
    slot_count = sp_count * per_peer
    all_coords, all_weight = (
        lax.all_gather(own_coords, "sp", axis=0, tiled=True),
        lax.all_gather(atom_weight, "sp", axis=0, tiled=True),
    )
    list_table = lax.all_gather(send_blocks, "sp", axis=0, tiled=True)
    column = lax.dynamic_index_in_dim(list_table, lax.axis_index("sp"), 1, keepdims=False)
    global_ids = (jnp.arange(sp_count, dtype=jnp.int32)[:, None] * blocks_dev + column).reshape(
        slot_count
    )
    slot_coords = all_coords[global_ids]
    slot_weight = all_weight[global_ids]
    table_coords = jnp.concatenate([own_coords, slot_coords], axis=0)
    table_weight = jnp.concatenate([atom_weight, slot_weight], axis=0)
    table_len = blocks_dev + slot_count
    tile_dev = tile_blocks.shape[0]
    list_len = tile_blocks.shape[1]
    group_count = tile_dev // 8
    live = (jnp.arange(list_len, dtype=jnp.int32)[None, :] < tile_counts[:, None]).astype(
        jnp.float32
    )
    grouped = (
        tile_blocks.reshape(group_count, 8, list_len),
        live.reshape(group_count, 8, list_len),
        centers.reshape(group_count, 8, 3, 128),
        inv_width.reshape(group_count, 8, 128),
    )

    def first_pass(packed):
        lists_here, live_here, centre_here, rate_here = packed
        block_coords = table_coords[lists_here]
        block_weight = table_weight[lists_here] * live_here[:, :, None]
        return jax.vmap(model_intersection)(block_coords, block_weight, centre_here, rate_here)

    model = lax.map(first_pass, grouped).reshape(tile_dev, 128)
    rep_count = lax.axis_size("rep")
    mean_model = lax.psum(model, "rep") / rep_count
    pull_rate = (mean_model - density) / variance * inv_width

    def second_pass(carry, packed):
        lists_here, live_here, centre_here, rate_here, pull_here = packed
        block_coords = table_coords[lists_here]
        block_weight = table_weight[lists_here] * live_here[:, :, None]
        pulls = jax.vmap(restraint_pull)(
            block_coords, block_weight, centre_here, rate_here, pull_here
        )
        return (carry.at[lists_here.reshape(-1)].add(pulls.reshape(-1, 384)), None)

    start_forces = jnp.zeros((table_len, 384), jnp.float32)
    table_forces, unused_out = lax.scan(
        second_pass, start_forces, grouped + (pull_rate.reshape(group_count, 8, 128),)
    )
    local_forces = table_forces[:blocks_dev]
    slot_forces = table_forces[blocks_dev:]
    whole_forces = (
        jnp.zeros((sp_count * blocks_dev, 384), jnp.float32).at[global_ids].add(slot_forces)
    )
    own_forces = local_forces + lax.psum_scatter(
        whole_forces, "sp", scatter_dimension=0, tiled=True
    )
    return (own_forces.reshape(1, blocks_dev, 3, 128), mean_model)


def solution(mesh):
    return jax.shard_map(
        local,
        mesh=mesh,
        in_specs=(
            P("rep", "sp", None, None),
            P("sp", None),
            P("sp", None, None),
            P("sp", None),
            P("sp", None),
            P("sp", None),
            P("sp", None),
            P("sp"),
            P("sp", None, None),
        ),
        out_specs=(P("rep", "sp", None, None), P("sp", None)),
        check_vma=False,
    )
```

profile of v0, /device:TPU:0, one launch (start us, length us, event | category | flops | bytes accessed | tf_op | source)
XLA Modules:
  0.0 677.6 jit_solution(9335107559699038428)
XLA Ops:
  12.5 25.2 %all_gather.10 = s32[16,16,16]{2,1,0:T(8,128)S(1)} all-gather(s32[1,16,16]{2,1,0:T(8,128)} %param.21), channel_id=1, replica_groups=mesh['rep'=8,'sp'=16] {'sp'}, dimensions={0}, use_global_device_ids=true | all-gather | bytes 17408 | tf_op jit(solution)/shard_map/all_gather | solution.py:51
  41.2 23.2 %all-gather.4.cloned.1.call-done = f32[8192,128]{1,0:T(8,128)} async-done(((f32[512,128]{1,0:T(8,128)}), f32[8192,128]{1,0:T(8,128)}) %all-gather.4.cloned.1.call-update) | async-done | bytes 4194320 | tf_op jit(solution)/shard_map/all_gather | solution.py:49
  64.5 2.9 gather_fusion.4
  67.4 89.5 %all-gather.6.cloned.1.call-done = f32[1,8192,3,128]{3,0,2,1:T(1,128)} async-done(((f32[1,512,3,128]{3,0,2,1:T(1,128)}), f32[1,8192,3,128]{3,0,2,1:T(1,128)}) %all-gather.6.cloned.1.call-update) | async-done | bytes 12582928 | tf_op jit(solution)/shard_map/all_gather | solution.py:48
  156.9 9.9 %copy.51 = f32[1,8192,3,128]{3,1,2,0:T(8,128)} copy(f32[1,8192,3,128]{3,0,2,1:T(1,128)} %all-gather.6.cloned.1.call-done) | data formatting | bytes 25165824 | tf_op jit(solution)/shard_map/all_gather | solution.py:48
  166.9 18.1 %copy.32 = f32[8192,3,128]{2,1,0:T(4,128)} copy(f32[8192,3,128]{2,0,1:T(8,128)} %bitcast.157) | data formatting | bytes 25165824 | tf_op jit(solution)/shard_map/all_gather | solution.py:48
  184.9 6.8 %gather_fusion.5 = f32[256,3,128]{2,1,0:T(4,128)S(1)} fusion(f32[8192,3,128]{2,1,0:T(4,128)} %copy.32, s32[1024]{0:T(1024)S(1)} %pad_clamp_fusion.2), kind=kCustom, calls=%fused_computation.5 | custom fusion | bytes 787456 | tf_op jit(solution)/shard_map/gather | solution.py:56
  192.1 170.8 %while.20 = (s32[]{:T(128)}, f32[4,8,128]{2,1,0:T(8,128)}, f32[4,8,128]{2,1,0:T(8,128)}, s32[4,8,32]{2,1,0:T(8,128)}, f32[768,3,128]{2,1,0:T(4,128)S(1)}, /*inde...) while((s32[]{:T(128)}, f32[4,8,128]{2,1,0:T(8,128)}, ...), condition=%wide.region_1.2_spmd, body=%wide.region_0.1_spmd.sunk | while | flops 88115968 | bytes 36276844 | solution.py:80
  195.7 9.9 %multiply_exponential_fusion.13 = f32[8,128,32,128]{3,2,1,0:T(8,128)} fusion(f32[8,128]{1,0:T(8,128)S(1)} %bitcast.179, f32[8,32,128]{2,1,0:T(8,128)S(1)} %bitcast.164, f32[8,128]{1,0:T(8,128)S(1)} %bitcast.180, f32[8,32,128]{2,1,0:T(8,128)S(1)} %bitcast.163, f32[8,128]{1,0:T(8,128)S(1)} %bitcast.178, f32[8,32,128]{2,1,0:T(8,128)S(1)} %bitcast.162, ...), kind=kLoop, calls=%fused_computation.10.clone.1 | loop fusion | flops 37748736 | bytes 17186816 | tf_op jit(solution)/shard_map/while/body/eval_jaxpr/vmap()/exp | solution.py:13
  206.5 27.7 %fusion.55 = f32[8,1,128,1]{2,1,3,0:T(1,128)S(1)} fusion(f32[8,32,128,1]{2,3,1,0:T(1,128)S(1)} %bitcast.161, f32[8,128,32,128]{3,2,1,0:T(8,128)} %multiply_exponential_fusion.13), kind=kOutput, calls=%fused_computation.8.clone.1 | convolution fusion | flops 50331648 | bytes 16912384 | tf_op jit(solution)/shard_map/while/body/eval_jaxpr/vmap(gja,ja->g)/dot_general | solution.py:18
  238.4 9.9 %multiply_exponential_fusion.13 = f32[8,128,32,128]{3,2,1,0:T(8,128)} fusion(f32[8,128]{1,0:T(8,128)S(1)} %bitcast.179, f32[8,32,128]{2,1,0:T(8,128)S(1)} %bitcast.164, f32[8,128]{1,0:T(8,128)S(1)} %bitcast.180, f32[8,32,128]{2,1,0:T(8,128)S(1)} %bitcast.163, f32[8,128]{1,0:T(8,128)S(1)} %bitcast.178, f32[8,32,128]{2,1,0:T(8,128)S(1)} %bitcast.162, ...), kind=kLoop, calls=%fused_computation.10.clone.1 | loop fusion | flops 37748736 | bytes 17186816 | tf_op jit(solution)/shard_map/while/body/eval_jaxpr/vmap()/exp | solution.py:13
  249.2 27.7 %fusion.55 = f32[8,1,128,1]{2,1,3,0:T(1,128)S(1)} fusion(f32[8,32,128,1]{2,3,1,0:T(1,128)S(1)} %bitcast.161, f32[8,128,32,128]{3,2,1,0:T(8,128)} %multiply_exponential_fusion.13), kind=kOutput, calls=%fused_computation.8.clone.1 | convolution fusion | flops 50331648 | bytes 16912384 | tf_op jit(solution)/shard_map/while/body/eval_jaxpr/vmap(gja,ja->g)/dot_general | solution.py:18
  281.1 9.9 %multiply_exponential_fusion.13 = f32[8,128,32,128]{3,2,1,0:T(8,128)} fusion(f32[8,128]{1,0:T(8,128)S(1)} %bitcast.179, f32[8,32,128]{2,1,0:T(8,128)S(1)} %bitcast.164, f32[8,128]{1,0:T(8,128)S(1)} %bitcast.180, f32[8,32,128]{2,1,0:T(8,128)S(1)} %bitcast.163, f32[8,128]{1,0:T(8,128)S(1)} %bitcast.178, f32[8,32,128]{2,1,0:T(8,128)S(1)} %bitcast.162, ...), kind=kLoop, calls=%fused_computation.10.clone.1 | loop fusion | flops 37748736 | bytes 17186816 | tf_op jit(solution)/shard_map/while/body/eval_jaxpr/vmap()/exp | solution.py:13
  291.8 27.7 %fusion.55 = f32[8,1,128,1]{2,1,3,0:T(1,128)S(1)} fusion(f32[8,32,128,1]{2,3,1,0:T(1,128)S(1)} %bitcast.161, f32[8,128,32,128]{3,2,1,0:T(8,128)} %multiply_exponential_fusion.13), kind=kOutput, calls=%fused_computation.8.clone.1 | convolution fusion | flops 50331648 | bytes 16912384 | tf_op jit(solution)/shard_map/while/body/eval_jaxpr/vmap(gja,ja->g)/dot_general | solution.py:18
  323.7 9.9 %multiply_exponential_fusion.13 = f32[8,128,32,128]{3,2,1,0:T(8,128)} fusion(f32[8,128]{1,0:T(8,128)S(1)} %bitcast.179, f32[8,32,128]{2,1,0:T(8,128)S(1)} %bitcast.164, f32[8,128]{1,0:T(8,128)S(1)} %bitcast.180, f32[8,32,128]{2,1,0:T(8,128)S(1)} %bitcast.163, f32[8,128]{1,0:T(8,128)S(1)} %bitcast.178, f32[8,32,128]{2,1,0:T(8,128)S(1)} %bitcast.162, ...), kind=kLoop, calls=%fused_computation.10.clone.1 | loop fusion | flops 37748736 | bytes 17186816 | tf_op jit(solution)/shard_map/while/body/eval_jaxpr/vmap()/exp | solution.py:13
  334.5 27.7 %fusion.55 = f32[8,1,128,1]{2,1,3,0:T(1,128)S(1)} fusion(f32[8,32,128,1]{2,3,1,0:T(1,128)S(1)} %bitcast.161, f32[8,128,32,128]{3,2,1,0:T(8,128)} %multiply_exponential_fusion.13), kind=kOutput, calls=%fused_computation.8.clone.1 | convolution fusion | flops 50331648 | bytes 16912384 | tf_op jit(solution)/shard_map/while/body/eval_jaxpr/vmap(gja,ja->g)/dot_general | solution.py:18
  362.9 25.6 %psum.7 = f32[32,128]{1,0:T(8,128)S(1)} all-reduce(f32[32,128]{1,0:T(8,128)} %bitcast.192), channel_id=1, replica_groups=mesh['rep'=8,'sp'=16] {'rep'}, use_global_device_ids=true, to_apply=%region_2.3 | all-reduce | flops 4096 | bytes 32768 | tf_op jit(solution)/shard_map/psum | solution.py:82
  390.9 177.6 %while.21 = (s32[]{:T(128)}, f32[768,384]{1,0:T(8,128)}, s32[4,8,32]{2,1,0:T(8,128)}, f32[768,128]{1,0:T(8,128)S(1)}, f32[4,8,32]{2,1,0:T(8,128)S(1)}, /*index=5...) while((s32[]{:T(128)}, f32[768,384]{1,0:T(8,128)}, ...), condition=%wide.region_5.6_spmd, body=%wide.region_3.5_spmd.sunk | while | flops 277289472 | bytes 5913725 | solution.py:95
  415.9 15.2 %fusion.61 = f32[8,1,32,128]{3,1,2,0:T(1,128)} fusion(f32[8,128,1,1]{1,2,3,0:T(1,128)S(1)} %bitcast.184, f32[8,128]{1,0:T(8,128)S(1)} %bitcast.187, f32[8,32,128]{2,1,0:T(8,128)S(1)} %bitcast.171, f32[8,128]{1,0:T(8,128)S(1)} %bitcast.189, f32[8,32,128]{2,1,0:T(8,128)S(1)} %bitcast.173, f32[8,128]{1,0:T(8,128)S(1)} %bitcast.185, ...), kind=kOutput, calls=%fused_computation.20.clone.1 | convolution fusion | flops 88080384 | bytes 544768 | tf_op jit(solution)/shard_map/while/body/eval_jaxpr/vmap(gja,g->ja)/dot_general | solution.py:23
  431.9 14.8 %fusion.63 = f32[8,32,3,128]{3,2,1,0:T(4,128)S(1)} fusion(f32[8,128]{1,0:T(8,128)S(1)} %bitcast.188, f32[8,32,128]{2,1,0:T(8,128)S(1)} %bitcast.172, f32[8,128]{1,0:T(8,128)S(1)} %bitcast.190, f32[8,32,128]{2,1,0:T(8,128)S(1)} %bitcast.174, f32[8,128]{1,0:T(8,128)S(1)} %bitcast.186, f32[8,32,128]{2,1,0:T(8,128)S(1)} %bitcast.170, ...), kind=kOutput, calls=%fused_computation.37.clone.1 | convolution fusion | flops 189041664 | bytes 1474560 | tf_op jit(solution)/shard_map/while/body/eval_jaxpr/vmap(gja,cg->jca)/dot_general | solution.py:24
  446.8 4.4 scatter_custom_fusion.7
  454.8 15.2 %fusion.61 = f32[8,1,32,128]{3,1,2,0:T(1,128)} fusion(f32[8,128,1,1]{1,2,3,0:T(1,128)S(1)} %bitcast.184, f32[8,128]{1,0:T(8,128)S(1)} %bitcast.187, f32[8,32,128]{2,1,0:T(8,128)S(1)} %bitcast.171, f32[8,128]{1,0:T(8,128)S(1)} %bitcast.189, f32[8,32,128]{2,1,0:T(8,128)S(1)} %bitcast.173, f32[8,128]{1,0:T(8,128)S(1)} %bitcast.185, ...), kind=kOutput, calls=%fused_computation.20.clone.1 | convolution fusion | flops 88080384 | bytes 544768 | tf_op jit(solution)/shard_map/while/body/eval_jaxpr/vmap(gja,g->ja)/dot_general | solution.py:23
  470.9 14.8 %fusion.63 = f32[8,32,3,128]{3,2,1,0:T(4,128)S(1)} fusion(f32[8,128]{1,0:T(8,128)S(1)} %bitcast.188, f32[8,32,128]{2,1,0:T(8,128)S(1)} %bitcast.172, f32[8,128]{1,0:T(8,128)S(1)} %bitcast.190, f32[8,32,128]{2,1,0:T(8,128)S(1)} %bitcast.174, f32[8,128]{1,0:T(8,128)S(1)} %bitcast.186, f32[8,32,128]{2,1,0:T(8,128)S(1)} %bitcast.170, ...), kind=kOutput, calls=%fused_computation.37.clone.1 | convolution fusion | flops 189041664 | bytes 1474560 | tf_op jit(solution)/shard_map/while/body/eval_jaxpr/vmap(gja,cg->jca)/dot_general | solution.py:24
  485.8 4.4 scatter_custom_fusion.7
  493.8 15.2 %fusion.61 = f32[8,1,32,128]{3,1,2,0:T(1,128)} fusion(f32[8,128,1,1]{1,2,3,0:T(1,128)S(1)} %bitcast.184, f32[8,128]{1,0:T(8,128)S(1)} %bitcast.187, f32[8,32,128]{2,1,0:T(8,128)S(1)} %bitcast.171, f32[8,128]{1,0:T(8,128)S(1)} %bitcast.189, f32[8,32,128]{2,1,0:T(8,128)S(1)} %bitcast.173, f32[8,128]{1,0:T(8,128)S(1)} %bitcast.185, ...), kind=kOutput, calls=%fused_computation.20.clone.1 | convolution fusion | flops 88080384 | bytes 544768 | tf_op jit(solution)/shard_map/while/body/eval_jaxpr/vmap(gja,g->ja)/dot_general | solution.py:23
  509.8 14.8 %fusion.63 = f32[8,32,3,128]{3,2,1,0:T(4,128)S(1)} fusion(f32[8,128]{1,0:T(8,128)S(1)} %bitcast.188, f32[8,32,128]{2,1,0:T(8,128)S(1)} %bitcast.172, f32[8,128]{1,0:T(8,128)S(1)} %bitcast.190, f32[8,32,128]{2,1,0:T(8,128)S(1)} %bitcast.174, f32[8,128]{1,0:T(8,128)S(1)} %bitcast.186, f32[8,32,128]{2,1,0:T(8,128)S(1)} %bitcast.170, ...), kind=kOutput, calls=%fused_computation.37.clone.1 | convolution fusion | flops 189041664 | bytes 1474560 | tf_op jit(solution)/shard_map/while/body/eval_jaxpr/vmap(gja,cg->jca)/dot_general | solution.py:24
  524.7 4.4 scatter_custom_fusion.7
  532.8 15.2 %fusion.61 = f32[8,1,32,128]{3,1,2,0:T(1,128)} fusion(f32[8,128,1,1]{1,2,3,0:T(1,128)S(1)} %bitcast.184, f32[8,128]{1,0:T(8,128)S(1)} %bitcast.187, f32[8,32,128]{2,1,0:T(8,128)S(1)} %bitcast.171, f32[8,128]{1,0:T(8,128)S(1)} %bitcast.189, f32[8,32,128]{2,1,0:T(8,128)S(1)} %bitcast.173, f32[8,128]{1,0:T(8,128)S(1)} %bitcast.185, ...), kind=kOutput, calls=%fused_computation.20.clone.1 | convolution fusion | flops 88080384 | bytes 544768 | tf_op jit(solution)/shard_map/while/body/eval_jaxpr/vmap(gja,g->ja)/dot_general | solution.py:23
  548.8 14.8 %fusion.63 = f32[8,32,3,128]{3,2,1,0:T(4,128)S(1)} fusion(f32[8,128]{1,0:T(8,128)S(1)} %bitcast.188, f32[8,32,128]{2,1,0:T(8,128)S(1)} %bitcast.172, f32[8,128]{1,0:T(8,128)S(1)} %bitcast.190, f32[8,32,128]{2,1,0:T(8,128)S(1)} %bitcast.174, f32[8,128]{1,0:T(8,128)S(1)} %bitcast.186, f32[8,32,128]{2,1,0:T(8,128)S(1)} %bitcast.170, ...), kind=kOutput, calls=%fused_computation.37.clone.1 | convolution fusion | flops 189041664 | bytes 1474560 | tf_op jit(solution)/shard_map/while/body/eval_jaxpr/vmap(gja,cg->jca)/dot_general | solution.py:24
  563.7 4.4 scatter_custom_fusion.7
  568.5 7.9 %scatter_custom_fusion.1 = f32[8192,384]{1,0:T(8,128)} fusion(s32[256]{0:T(256)} %bitcast.194, f32[]{:T(128)} %constant.35.clone.1, f32[768,384]{1,0:T(8,128)} %get-tuple-element.92), kind=kCustom, calls=%fused_computation.54 | custom fusion | flops 98304 | bytes 12976640 | tf_op jit(solution)/shard_map/scatter-add | solution.py:101
  576.4 91.9 %reduce-scatter.2.cloned.1.call-done = f32[512,384]{1,0:T(8,128)} async-done(((f32[8192,384]{1,0:T(8,128)}), f32[512,384]{1,0:T(8,128)}) %reduce-scatter.2.cloned.1.call-update) | async-done | bytes 786448 | tf_op jit(solution)/shard_map/reduce_scatter | solution.py:103
  (143 shorter events, 52.5 us)
Async XLA Ops:
  7.2 57.3 %all-gather.4.cloned.1.call-start = ((), (), s32[]{:S(2)}) async-start(), calls=%async_computation.1 | async-start | bytes 4456448 | tf_op jit(solution)/shard_map/all_gather | solution.py:49
  7.9 149.0 %all-gather.6.cloned.1.call-start = ((), (), s32[]{:S(2)}) async-start(), calls=%async_computation.3 | async-start | bytes 13369344 | tf_op jit(solution)/shard_map/all_gather | solution.py:48
  10.8 657.5 %reduce-scatter.2.cloned.1.call-start = ((), (), s32[]{:S(2)}) async-start(), calls=%async_computation.2 | async-start | bytes 13369344 | tf_op jit(solution)/shard_map/reduce_scatter | solution.py:103
  40.2 1.1 copy-start.3
  192.0 196.4 %copy-start.1 = (f32[32,128]{1,0:T(8,128)S(1)}, f32[32,128]{1,0:T(8,128)}, u32[]{:S(2)}) copy-start(f32[32,128]{1,0:T(8,128)} %param.18) | copy-start | bytes 49156
  192.0 196.4 %copy-start.2 = (f32[32,128]{1,0:T(8,128)S(1)}, f32[32,128]{1,0:T(8,128)}, u32[]{:S(2)}) copy-start(f32[32,128]{1,0:T(8,128)} %param.17) | copy-start | bytes 49156
  568.5 99.8 %copy-start = (f32[768,384]{1,0:T(8,128)S(1)}, f32[768,384]{1,0:T(8,128)}, u32[]{:S(2)}) copy-start(f32[768,384]{1,0:T(8,128)} %get-tuple-element.92) | copy-start | bytes 3538948
Sparse Core Ops, SparseCore 0:
  10.1 54.2 all-gather.3
  67.2 89.7 all-gather.5
  576.5 91.7 reduce-scatter.1
where the time goes:
time: 690 us; the launch traced here: 678 us
  matrix products  231 us (33%)
  waiting for transfers between devices  205 us (30%)
  other arithmetic  80.3 us (12%)
  local copies, waits for them, and re-layouts  74.4 us (11%)
  blocking collectives  50.7 us (7%)
  loops' own time  22 us (3%)
  between operations  14 us (2%)
    dot_general x4, matrix products, model_intersection(): jnp.einsum('gja,ja->g', kernel, block_weight, precision=lax.Precision.HIG...  111 us
    reduce_scatter x1, waiting for transfers between devices, local(): lax.psum_scatter(whole_forces, 'sp', scatter_dimension=0, tiled=True)  91.9 us
    all_gather x1, waiting for transfers between devices, local(): lax.all_gather(own_coords, 'sp', axis=0, tiled=True)  89.5 us
    dot_general x4, matrix products, restraint_pull(): jnp.einsum('gja,g->ja', kernel, pull_rate, precision=lax.Precision.HIGHEST)  60.7 us
    dot_general x4, matrix products, restraint_pull(): jnp.einsum('gja,cg->jca', kernel, pull_rate[None, :] * centre, precision=...  59.2 us
    exp x4, other arithmetic, gaussian_kernel(): return jnp.exp(-width_rate[:, None, None] * dist_sq)  39.8 us
    all_gather x2, local copies, waits for them, and re-layouts, local(): lax.all_gather(own_coords, 'sp', axis=0, tiled=True)  28 us
    psum x1, blocking collectives, local(): mean_model = lax.psum(model, 'rep') / rep_count  25.6 us
  transfers between devices with their start and end apart: 3, of which 3 were waited for; matrix products, arithmetic and copies ran while one was open for 2% of the time, Pallas kernels for 0%

commit v1 on v0

v1 whole, which is shorter than its diff:
```python
import functools

import jax
import jax.numpy as jnp
from jax import lax
from jax.experimental import pallas as pl
from jax.experimental.pallas import tpu as pltpu
from jax.sharding import PartitionSpec as P

MESH = pl.DeviceIdType.MESH
BF = jnp.bfloat16
F32 = jnp.float32
I32 = jnp.int32
VMEM = pl.BlockSpec(memory_space=pltpu.VMEM)
SMEM = pl.BlockSpec(memory_space=pltpu.SMEM)

OFFSETS = (1, 2, 3, 8, 13, 14, 15)
CAP = 16
OWN = 512
HALO = len(OFFSETS) * CAP
TABLE = OWN + HALO
DUMMY = TABLE
ROWS = TABLE + CAP
TILES = 32
LIST = 32
STEPS = TILES * LIST // 2
FLAT = STEPS + 64
DEPTH = 48
LOG2E = 1.4426950408889634


def params(limit_mib, collective_id=None):
    more = {} if collective_id is None else {"collective_id": collective_id, "has_side_effects": True}
    return pltpu.CompilerParams(vmem_limit_bytes=limit_mib << 20, **more)


def sp_peer(offset):
    return (lax.axis_index("rep"), lax.rem(lax.axis_index("sp") + offset, 16))


def greet(peers):
    barrier = pltpu.get_barrier_semaphore()
    for peer in peers:
        pl.semaphore_signal(barrier, inc=1, device_id=peer, device_id_type=MESH)
    pl.semaphore_wait(barrier, len(peers))


def halo_kernel(send_ref, coords_ref, weight_ref, out_ref, pack, send_sem, recv_sem):
    me = lax.axis_index("sp")
    greet([sp_peer(o) for o in OFFSETS])
    copies = []
    for p, offset in enumerate(OFFSETS):
        to = lax.rem(me + 16 - offset, 16)
        for k in range(CAP):
            b = send_ref[to, k]
            pack[p * CAP + k, 0:3, :] = coords_ref[b]
            pack[p * CAP + k, 3:4, :] = weight_ref[pl.ds(b, 1), :]
        copy = pltpu.make_async_remote_copy(
            src_ref=pack.at[pl.ds(p * CAP, CAP)],
            dst_ref=out_ref.at[pl.ds(p * CAP, CAP)],
            send_sem=send_sem.at[p],
            recv_sem=recv_sem.at[p],
            device_id=(lax.axis_index("rep"), to),
            device_id_type=MESH,
        )
        copy.start()
        copies.append(copy)
    for copy in copies:
        copy.wait()


def halo(send, coords, weight):
    return pl.pallas_call(
        halo_kernel,
        out_shape=jax.ShapeDtypeStruct((HALO, 4, 128), F32),
        in_specs=[SMEM, VMEM, VMEM],
        out_specs=VMEM,
        scratch_shapes=[
            pltpu.VMEM((HALO, 4, 128), F32),
            pltpu.SemaphoreType.DMA((len(OFFSETS),)),
            pltpu.SemaphoreType.DMA((len(OFFSETS),)),
        ],
        compiler_params=params(16, 0),
        name="halo",
    )(send, coords, weight)


def pieces(x):
    hi = x.astype(BF).astype(F32)
    rest = x - hi
    mid = rest.astype(BF).astype(F32)
    return hi, mid, rest - mid


def features(xyz):
    square = jnp.sum(xyz * xyz, axis=0, keepdims=True)
    hi, mid, lo = pieces(jnp.concatenate([xyz, square], axis=0))
    return jnp.concatenate([hi, mid, hi, lo], axis=0).astype(BF)


def tile_rates(centers, rate):
    slope = rate * LOG2E
    rows = jnp.concatenate([2.0 * slope * centers, -slope], axis=0)
    hi, mid, lo = pieces(rows)
    size = jnp.sum(centers * centers, axis=0, keepdims=True)
    c_hi, c_mid, c_lo = pieces(-slope * size)
    zero8 = jnp.zeros((8, 128), F32)
    zero13 = jnp.zeros((13, 128), F32)
    return jnp.concatenate([hi, hi, mid, hi, lo, mid, zero8, c_hi, c_mid, c_lo, zero13], axis=0)


def unpack(word):
    return lax.shift_right_logical(word, 20), lax.shift_right_logical(word, 10) & 1023, word & 1023


def exponents(flat, rates, feats, at, out_ref, slot):
    t, b1, b2 = unpack(flat[at])
    pair = jnp.concatenate([feats[b1], feats[b2]], axis=1)
    ones = jnp.ones((16, 256), BF)
    out_ref[slot] = jnp.dot(
        rates[t], jnp.concatenate([pair, pair, ones], axis=0), preferred_element_type=F32
    )


def model_kernel(
    turns, depth, count, flat, coords, weight, received, centers, width,
    model_ref, rates, feats, weights, power, total,
):
    def own(b, carry):
        feats[b] = features(coords[b])
        return carry

    lax.fori_loop(0, OWN, own, 0, unroll=8)

    def slot(b, carry):
        feats[OWN + b] = features(received[b, 0:3, :])
        weights[pl.ds(OWN + b, 1), :] = received[b, 3:4, :]
        return carry

    lax.fori_loop(0, HALO, slot, 0, unroll=8)
    weights[0:OWN, :] = weight[...]
    for b in range(TABLE, ROWS):
        feats[b] = jnp.zeros((16, 128), BF)
    weights[TABLE:ROWS, :] = jnp.zeros((ROWS - TABLE, 128), F32)

    def tile(t, carry):
        rows = tile_rates(centers[t], width[pl.ds(t, 1), :])
        rates[t] = jnp.transpose(rows).astype(BF)
        total[t] = jnp.zeros((128, 128), F32)
        return carry

    lax.fori_loop(0, TILES, tile, 0, unroll=2)

    def add(at, src):
        t, b1, b2 = unpack(flat[at])
        k = jnp.exp2(power[src])
        total[t] += k[:, :128] * weights[pl.ds(b1, 1), :] + k[:, 128:] * weights[pl.ds(b2, 1), :]

    for d in range(depth):
        exponents(flat, rates, feats, d, power, d)

    def body(i, carry):
        first = turns * i
        for u in range(turns):
            exponents(flat, rates, feats, first + u + depth, power, (u + depth) % turns)
            add(first + u, u)
        return carry

    lax.fori_loop(0, (count[0] + turns - 1) // turns, body, 0)
    for t in range(TILES):
        model_ref[t, :] = jnp.sum(total[t], axis=-1)


def model_pass(count, flat, coords, weight, received, centers, width):
    turns, depth = 16, 4
    return pl.pallas_call(
        functools.partial(model_kernel, turns, depth),
        out_shape=(
            jax.ShapeDtypeStruct((TILES, 128), F32),
            jax.ShapeDtypeStruct((TILES, 128, DEPTH), BF),
            jax.ShapeDtypeStruct((ROWS, 16, 128), BF),
        ),
        in_specs=[SMEM, SMEM, VMEM, VMEM, VMEM, VMEM, VMEM],
        out_specs=(VMEM, VMEM, VMEM),
        scratch_shapes=[
            pltpu.VMEM((ROWS, 128), F32),
            pltpu.VMEM((turns, 128, 256), F32),
            pltpu.VMEM((TILES, 128, 128), F32),
        ],
        compiler_params=params(40),
        name="model_pass",
    )(count, flat, coords, weight, received, centers, width)


def replica_kernel(
    model, centers, width, density, variance, mean_ref, pull_ref, slots, send_sem, recv_sem
):
    rep, sp = lax.axis_index("rep"), lax.axis_index("sp")
    greet([(lax.rem(rep + d, 8), sp) for d in range(1, 8)])
    copies = []
    for d in range(1, 8):
        copy = pltpu.make_async_remote_copy(
            src_ref=model,
            dst_ref=slots.at[rep],
            send_sem=send_sem.at[d],
            recv_sem=recv_sem.at[d],
            device_id=(lax.rem(rep + d, 8), sp),
            device_id_type=MESH,
        )
        copy.start()
        copies.append(copy)
    slots[rep] = model[...]
    for copy in copies:
        copy.wait()
    sum_ = slots[0]
    for r in range(1, 8):
        sum_ = sum_ + slots[r]
    mean = sum_ * 0.125
    mean_ref[...] = mean
    rate = (mean - density[...]) / variance[...] * width[...]
    for t in range(TILES):
        row = rate[t : t + 1, :]
        four = jnp.concatenate([row, row * centers[t]], axis=0)
        hi = four.astype(BF).astype(F32)
        rows = jnp.concatenate([hi, four - hi, jnp.zeros((8, 128), F32)], axis=0).astype(BF)
        pull_ref[t] = jnp.concatenate([rows, rows], axis=1)


def replica_sum(model, centers, width, density, variance):
    return pl.pallas_call(
        replica_kernel,
        out_shape=(
            jax.ShapeDtypeStruct((TILES, 128), F32),
            jax.ShapeDtypeStruct((TILES, 16, 256), BF),
        ),
        in_specs=[VMEM] * 5,
        out_specs=(VMEM, VMEM),
        scratch_shapes=[
            pltpu.VMEM((8, TILES, 128), F32),
            pltpu.SemaphoreType.DMA((8,)),
            pltpu.SemaphoreType.DMA((8,)),
        ],
        compiler_params=params(16, 1),
        name="replica_sum",
    )(model, centers, width, density, variance)


def force_kernel(
    turns, depth, count, flat, rates, feats, pulls, coords, weight, received,
    own_ref, slot_ref, moments, power, split,
):
    def clear(b, carry):
        moments[b] = jnp.zeros((8, 128), F32)
        return carry

    lax.fori_loop(0, ROWS, clear, 0, unroll=8)

    def raise_(src):
        k = jnp.exp2(power[src])
        hi = k.astype(BF)
        split[src, :128] = hi
        split[src, 128:] = (k - hi.astype(F32)).astype(BF)

    def reduce(at, src):
        t, b1, b2 = unpack(flat[at])
        both = jnp.dot(pulls[t], split[src], preferred_element_type=F32)
        moments[b1] += both[:8, :128]
        moments[b2] += both[:8, 128:]

    for d in range(2 * depth):
        exponents(flat, rates, feats, d, power, d)
    for d in range(depth):
        raise_(d)

    def body(i, carry):
        first = turns * i
        for u in range(turns):
            exponents(flat, rates, feats, first + u + 2 * depth, power, (u + 2 * depth) % turns)
            raise_((u + depth) % turns)
            reduce(first + u, u)
        return carry

    lax.fori_loop(0, (count[0] + turns - 1) // turns, body, 0)

    def pull(eight, xyz, weights):
        four = eight[0:4] + eight[4:8]
        return 2.0 * weights * (xyz * four[0:1] - four[1:4])

    def own(b, carry):
        own_ref[b] = pull(moments[b], coords[b], weight[pl.ds(b, 1), :])
        return carry

    lax.fori_loop(0, OWN, own, 0, unroll=8)

    def slot(b, carry):
        got = received[b]
        slot_ref[b, 0:3, :] = pull(moments[OWN + b], got[0:3], got[3:4])
        return carry

    lax.fori_loop(0, HALO, slot, 0, unroll=8)


def force_pass(count, flat, rates, feats, pulls, coords, weight, received):
    turns, depth = 16, 2
    return pl.pallas_call(
        functools.partial(force_kernel, turns, depth),
        out_shape=(
            jax.ShapeDtypeStruct((OWN, 3, 128), F32),
            jax.ShapeDtypeStruct((HALO, 4, 128), F32),
        ),
        in_specs=[SMEM, SMEM] + [VMEM] * 6,
        out_specs=(VMEM, VMEM),
        scratch_shapes=[
            pltpu.VMEM((ROWS, 8, 128), F32),
            pltpu.VMEM((turns, 128, 256), F32),
            pltpu.VMEM((turns, 256, 256), BF),
        ],
        compiler_params=params(40),
        name="force_pass",
    )(count, flat, rates, feats, pulls, coords, weight, received)


def return_kernel(slot_ref, out_ref, send_sem, recv_sem):
    greet([sp_peer(o) for o in OFFSETS])
    copies = []
    for p, offset in enumerate(OFFSETS):
        copy = pltpu.make_async_remote_copy(
            src_ref=slot_ref.at[pl.ds(p * CAP, CAP)],
            dst_ref=out_ref.at[pl.ds(p * CAP, CAP)],
            send_sem=send_sem.at[p],
            recv_sem=recv_sem.at[p],
            device_id=sp_peer(offset),
            device_id_type=MESH,
        )
        copy.start()
        copies.append(copy)
    for copy in copies:
        copy.wait()


def return_forces(slots):
    return pl.pallas_call(
        return_kernel,
        out_shape=jax.ShapeDtypeStruct((HALO, 4, 128), F32),
        in_specs=[VMEM],
        out_specs=VMEM,
        scratch_shapes=[
            pltpu.SemaphoreType.DMA((len(OFFSETS),)),
            pltpu.SemaphoreType.DMA((len(OFFSETS),)),
        ],
        compiler_params=params(16, 2),
        name="return_forces",
    )(slots)


def merge_kernel(send_ref, own_ref, back_ref, out_ref):
    out_ref[...] = own_ref[...]
    me = lax.axis_index("sp")
    for p, offset in enumerate(OFFSETS):
        to = lax.rem(me + 16 - offset, 16)
        for k in range(CAP):
            b = send_ref[to, k]
            out_ref[b] += back_ref[p * CAP + k, 0:3, :]


def merge(send, own, back):
    return pl.pallas_call(
        merge_kernel,
        out_shape=jax.ShapeDtypeStruct((OWN, 3, 128), F32),
        in_specs=[SMEM, VMEM, VMEM],
        out_specs=VMEM,
        compiler_params=params(16),
        name="merge",
    )(send, own, back)


def flat_list(tile_blocks, tile_counts):
    me = lax.axis_index("sp")
    slot = tile_blocks - OWN
    offset = (slot // CAP - me) & 15
    place = jnp.where(offset < 4, offset - 1, jnp.where(offset == 8, 3, offset - 9))
    ids = jnp.where(slot < 0, tile_blocks, OWN + place * CAP + (slot & (CAP - 1)))
    ids = jnp.where(jnp.arange(LIST, dtype=I32)[None, :] < tile_counts[:, None], ids, DUMMY)
    ids = ids.reshape(TILES, LIST // 2, 2)
    words = (jnp.arange(TILES, dtype=I32)[:, None] << 20) | (ids[:, :, 0] << 10) | ids[:, :, 1]
    steps = (tile_counts + 1) >> 1
    earlier = jnp.arange(TILES, dtype=I32)[None, :] < jnp.arange(TILES, dtype=I32)[:, None]
    base = jnp.sum(jnp.where(earlier, steps[None, :], 0), axis=1)
    at = jnp.arange(LIST // 2, dtype=I32)[None, :]
    place = jnp.where(at < steps[:, None], base[:, None] + at, -1).reshape(STEPS)
    hit = place[None, :] == jnp.arange(FLAT, dtype=I32)[:, None]
    count = jnp.sum(steps)
    flat = jnp.sum(jnp.where(hit, words.reshape(STEPS)[None, :], 0), axis=1)
    flat = jnp.where(jnp.arange(FLAT, dtype=I32) < count, flat, (DUMMY << 10) | DUMMY)
    return count[None], flat


def local(
    coords, atom_weight, centers, inv_width, density, variance, tile_blocks, tile_counts, send_blocks
):
    own, send = coords[0], send_blocks[0]
    received = halo(send, own, atom_weight)
    count, flat = flat_list(tile_blocks, tile_counts)
    model, rates, feats = model_pass(count, flat, own, atom_weight, received, centers, inv_width)
    mean, pulls = replica_sum(model, centers, inv_width, density, variance)
    forces, slots = force_pass(count, flat, rates, feats, pulls, own, atom_weight, received)
    back = return_forces(slots)
    return merge(send, forces, back)[None], mean


def solution(mesh):
    return jax.shard_map(
        local,
        mesh=mesh,
        in_specs=(
            P("rep", "sp", None, None),
            P("sp", None),
            P("sp", None, None),
            P("sp", None),
            P("sp", None),
            P("sp", None),
            P("sp", None),
            P("sp"),
            P("sp", None, None),
        ),
        out_specs=(P("rep", "sp", None, None), P("sp", None)),
        check_vma=False,
    )
```

time: 690 us -> 77.9 us (0.11); the launches traced: 678 us -> 77.5 us
  matrix products: 231 us -> 0 us
  waiting for transfers between devices: 205 us -> 0 us
  other arithmetic: 80.3 us -> 3.06 us
  local copies, waits for them, and re-layouts: 74.4 us -> 5.44 us
  Pallas kernels: 0 us -> 68.2 us
  blocking collectives: 50.7 us -> 0 us
  loops' own time: 22 us -> 0 us
  between operations: 14 us -> 0.81 us
    dot_general x12 -> x0, matrix products: 231 us -> none  [the longest x4 111 us: model_intersection(): jnp.einsum('gja,ja->g', kernel, block_weight, precision=lax.Precision.HIG...]
    all_gather x2 -> x0, waiting for transfers between devices: 113 us -> none  [the longest x1 89.5 us: local(): lax.all_gather(own_coords, 'sp', axis=0, tiled=True)]
    reduce_scatter x1 -> x0, waiting for transfers between devices: 91.9 us -> none  [local(): lax.psum_scatter(whole_forces, 'sp', scatter_dimension=0, tiled=True)]
    pallas_call x0 -> x6, Pallas kernels: none -> 68.2 us  [the longest x1 18.3 us: force_pass(): pl.pallas_call(functools.partial(force_kernel, turns, depth), out_shape=(...]
    exp x4 -> x0, other arithmetic: 39.8 us -> none  [gaussian_kernel(): return jnp.exp(-width_rate[:, None, None] * dist_sq)]
    all_gather x2 -> x0, local copies, waits for them, and re-layouts: 28 us -> none  [local(): lax.all_gather(own_coords, 'sp', axis=0, tiled=True)]
    psum x1 -> x0, blocking collectives: 25.6 us -> none  [local(): mean_model = lax.psum(model, 'rep') / rep_count]
    scatter-add x5 -> x0, other arithmetic: 25.6 us -> none  [the longest x4 17.7 us: second_pass(): return (carry.at[lists_here.reshape(-1)].add(pulls.reshape(-1, 384)), None)]
  transfers between devices with their start and end apart: 3 -> 0, of which waited for: 3 -> 0; matrix products, arithmetic and copies ran while one was open for 2% -> 0% of each run, Pallas kernels for 0% -> 0%
where the time goes in v1:
time: 77.9 us; the launch traced here: 77.5 us
  Pallas kernels  68.2 us (88%)
  local copies, waits for them, and re-layouts  5.44 us (7%)
  other arithmetic  3.06 us (4%)
  between operations  0.81 us (1%)
    pallas_call x1, Pallas kernels, force_pass(): pl.pallas_call(functools.partial(force_kernel, turns, depth), out_shape=(...  18.3 us
    pallas_call x1, Pallas kernels, model_pass(): pl.pallas_call(functools.partial(model_kernel, turns, depth), out_shape=(...  15.7 us
    pallas_call x1, Pallas kernels, return_forces(): pl.pallas_call(return_kernel, out_shape=jax.ShapeDtypeStruct((HALO, 4, 12...  14 us
    pallas_call x1, Pallas kernels, halo(): pl.pallas_call(halo_kernel, out_shape=jax.ShapeDtypeStruct((HALO, 4, 128)...  11.9 us
    pallas_call x1, Pallas kernels, replica_sum(): pl.pallas_call(replica_kernel, out_shape=(jax.ShapeDtypeStruct((TILES, 12...  7.04 us
    unnamed x15, local copies, waits for them, and re-layouts  4.88 us

profile of v1, /device:TPU:0, one launch (start us, length us, event | category | flops | bytes accessed | tf_op | source)
XLA Modules:
  0.0 77.5 jit_solution(17158692477594782540)
XLA Ops:
  0.6 0.0 copy-start
  0.6 0.0 copy-start.2
  0.7 1.3 %add_shift-right-arithmetic_fusion = (s32[32]{0:T(128)S(1)}, s32[]{:T(128)}) fusion(s32[32]{0:T(128)} %param.16), kind=kLoop, calls=%fused_computation.23 | loop fusion | flops 95 | bytes 260 | tf_op jit(solution)/shard_map/shift_right_arithmetic | solution.py:386
  2.0 0.1 select_reduce_fusion.1
  2.1 0.1 add_select_fusion.1
  2.2 0.1 select_n.44
  2.2 0.1 or.21
  2.3 0.1 or.22
  2.4 0.8 %copy.31 = s32[32,32]{0,1:T(8,128)S(1)} copy(s32[32,32]{1,0:T(8,128)} %param.15) | data formatting | bytes 8192 | tf_op args[6]
  3.2 0.7 select_select_fusion
  3.9 0.1 copy.34
  4.0 0.1 shift_left.28
  4.1 0.1 copy.35
  4.1 0.1 squeeze.11
  4.2 0.2 select_reduce_fusion
  4.5 0.7 fusion.4.flat
  5.1 0.8 %copy.37.centers = f32[32,3,128]{2,1,0:T(4,128)S(1)} copy(f32[32,3,128]{2,0,1:T(8,128)} %param.11) | data formatting | bytes 98304 | tf_op args[2]
  6.0 1.7 %copy.42 = f32[1,512,3,128]{3,2,1,0:T(4,128)S(1)} copy(f32[1,512,3,128]{3,1,2,0:T(8,128)} %param.9) | data formatting | bytes 1572864 | tf_op args[0]
  7.6 0.0 copy-start.1
  7.6 0.0 copy-done
  7.7 0.0 copy-done.2
  7.7 11.9 %halo.1.received = f32[112,4,128]{2,1,0:T(4,128)S(1)} custom-call(s32[16,16]{1,0:T(8,128)S(1)} %bitcast.16, f32[512,3,128]{2,1,0:T(4,128)S(1)} %bitcast.12, f32[512,128]{1,0:T(8,128)S(1)} %copy-done), custom_call_target="tpu_custom_call" | custom-call | tf_op jit(solution)/shard_map/halo/pallas_call | solution.py:73
  19.6 0.0 copy-done.1
  19.6 0.0 copy-start.3
  19.6 0.0 copy-start.4
  19.6 15.7 %model_pass.1 = (f32[32,128]{1,0:T(8,128)S(1)}, bf16[32,128,48]{2,1,0:T(8,128)(2,1)S(1)}, bf16[640,16,128]{2,1,0:T(8,128)(2,1)S(1)}) custom-call(s32[1]{0:T(128)} %bitcast.1.count, s32[576]{0:T(1024)S(1)} %fusion.4.flat, f32[512,3,128]{2,1,0:T(4,128)S(1)} %bitcast.13, f32[512,128]{1,0:T(8,128)S(1)} %copy-done, f32[112,4,128]{2,1,0:T(4,128)S(1)} %halo.1.received, ...), custom_call_target="tpu_custom_call" | custom-call | tf_op jit(solution)/shard_map/model_pass/pallas_call | solution.py:176
  35.3 7.0 %replica_sum.1 = (f32[32,128]{1,0:T(8,128)S(1)}, bf16[32,16,256]{2,1,0:T(8,128)(2,1)S(1)}) custom-call(f32[32,128]{1,0:T(8,128)S(1)} %get-tuple-element.11.model, f32[32,3,128]{2,1,0:T(4,128)S(1)} %copy.37.centers, f32[32,128]{1,0:T(8,128)S(1)} %copy-done.1, f32[32,128]{1,0:T(8,128)S(1)} %copy-done.3, f32[32,128]{1,0:T(8,128)S(1)} %copy-done.4), custom_call_target="tpu_custom_call" | custom-call | tf_op jit(solution)/shard_map/replica_sum/pallas_call | solution.py:230
  42.3 18.3 %force_pass.1 = (f32[512,3,128]{2,1,0:T(4,128)S(1)}, f32[112,4,128]{2,1,0:T(4,128)S(1)}) custom-call(s32[1]{0:T(128)} %bitcast.1.count, s32[576]{0:T(1024)S(1)} %fusion.4.flat, bf16[32,128,48]{2,1,0:T(8,128)(2,1)S(1)} %get-tuple-element.9.rates, bf16[640,16,128]{2,1,0:T(8,128)(2,1)S(1)} %get-tuple-element.10.feats, ...), custom_call_target="tpu_custom_call" | custom-call | tf_op jit(solution)/shard_map/force_pass/pallas_call | solution.py:305
  60.6 14.0 %return_forces.1.back_ref = f32[112,4,128]{2,1,0:T(4,128)S(1)} custom-call(f32[112,4,128]{2,1,0:T(4,128)S(1)} %get-tuple-element.14.slot_ref), custom_call_target="tpu_custom_call" | custom-call | tf_op jit(solution)/shard_map/return_forces/pallas_call | solution.py:342
  74.7 1.3 %merge.1 = f32[512,3,128]{2,1,0:T(4,128)S(1)} custom-call(s32[16,16]{1,0:T(8,128)S(1)} %bitcast.17, f32[512,3,128]{2,1,0:T(4,128)S(1)} %get-tuple-element.13.own_ref, f32[112,4,128]{2,1,0:T(4,128)S(1)} %return_forces.1.back_ref), custom_call_target="tpu_custom_call" | custom-call | tf_op jit(solution)/shard_map/merge/pallas_call | solution.py:367
  76.0 0.9 %copy.39 = f32[1,512,3,128]{3,1,2,0:T(8,128)} copy(f32[1,512,3,128]{3,2,1,0:T(4,128)S(1)} %bitcast.15) | data formatting | bytes 1572864
  76.9 0.6 copy.44
  (6 shorter events, 0.0 us)
Async XLA Ops:
  0.6 7.0 %copy-start = (f32[512,128]{1,0:T(8,128)S(1)}, f32[512,128]{1,0:T(8,128)}, u32[]{:S(2)}) copy-start(f32[512,128]{1,0:T(8,128)} %weight.3) | copy-start | bytes 786436
  0.6 7.0 %copy-start.2 = (s32[1,16,16]{2,1,0:T(8,128)S(1)}, s32[1,16,16]{2,1,0:T(8,128)}, u32[]{:S(2)}) copy-start(s32[1,16,16]{2,1,0:T(8,128)} %param.17) | copy-start | bytes 3076
  7.6 11.9 %copy-start.1 = (f32[32,128]{1,0:T(8,128)S(1)}, f32[32,128]{1,0:T(8,128)}, u32[]{:S(2)}) copy-start(f32[32,128]{1,0:T(8,128)} %width.3) | copy-start | bytes 49156
  19.6 15.7 %copy-start.3 = (f32[32,128]{1,0:T(8,128)S(1)}, f32[32,128]{1,0:T(8,128)}, u32[]{:S(2)}) copy-start(f32[32,128]{1,0:T(8,128)} %density.1) | copy-start | bytes 49156
  19.6 15.7 %copy-start.4 = (f32[32,128]{1,0:T(8,128)S(1)}, f32[32,128]{1,0:T(8,128)}, u32[]{:S(2)}) copy-start(f32[32,128]{1,0:T(8,128)} %variance.1) | copy-start | bytes 49156

commit v2 on v1

v2 whole, which is shorter than its diff:
```python
import functools

import jax
import jax.numpy as jnp
from jax import lax
from jax.experimental import pallas as pl
from jax.experimental.pallas import tpu as pltpu
from jax.sharding import PartitionSpec as P

MESH = pl.DeviceIdType.MESH
BF = jnp.bfloat16
F32 = jnp.float32
I32 = jnp.int32
VMEM = pl.BlockSpec(memory_space=pltpu.VMEM)
SMEM = pl.BlockSpec(memory_space=pltpu.SMEM)

OFFSETS = (1, 2, 3, 8, 13, 14, 15)
CAP = 16
OWN = 512
HALO = len(OFFSETS) * CAP
TABLE = OWN + HALO
DUMMY = TABLE
ROWS = TABLE + CAP
TILES = 32
LIST = 32
STEPS = TILES * LIST // 2
FLAT = 640
SAVED = 320
BACK = 3 * CAP
DEPTH = 48
WORK = 32
RING = 8
LOG2E = 1.4426950408889634


def params(limit_mib, collective_id=None):
    more = {} if collective_id is None else {"collective_id": collective_id, "has_side_effects": True}
    return pltpu.CompilerParams(vmem_limit_bytes=limit_mib << 20, **more)


def sp_peer(offset):
    return (lax.axis_index("rep"), lax.rem(lax.axis_index("sp") + offset, 16))


def greet(peers):
    barrier = pltpu.get_barrier_semaphore()
    for peer in peers:
        pl.semaphore_signal(barrier, inc=1, device_id=peer, device_id_type=MESH)
    pl.semaphore_wait(barrier, len(peers))


def pieces(x):
    hi = x.astype(BF).astype(F32)
    rest = x - hi
    mid = rest.astype(BF).astype(F32)
    return hi, mid, rest - mid


def put_features(xyz, feats, first, lines, at):
    square = xyz[0] * xyz[0] + xyz[1] * xyz[1] + xyz[2] * xyz[2]
    for row, value in enumerate((*xyz, square)):
        hi, mid, lo = pieces(value)
        for group, piece in enumerate((hi, mid, hi, lo)):
            lines[pl.ds(at * 128 + 4 * group + row, 8, stride=16), :] = piece
    for b in range(8):
        feats[first + b] = lines[at * 128 + 16 * b : at * 128 + 16 * b + 16, :].astype(BF)


def put_rates(centers, width, rates, lines):
    slope = width[...] * LOG2E
    x = [centers[c] for c in range(3)]
    size = x[0] * x[0] + x[1] * x[1] + x[2] * x[2]
    zero = jnp.zeros((TILES, 128), F32)
    rows = [zero] * DEPTH
    for c, value in enumerate([2.0 * slope * x[0], 2.0 * slope * x[1], 2.0 * slope * x[2], -slope]):
        hi, mid, lo = pieces(value)
        for group, piece in enumerate((hi, hi, mid, hi, lo, mid)):
            rows[4 * group + c] = piece
    for at, piece in enumerate(pieces(-slope * size)):
        rows[32 + at] = piece
    for r in range(DEPTH):
        for q in range(TILES // 8):
            lines[pl.ds(8 * q * DEPTH + r, 8, stride=DEPTH), :] = rows[r][8 * q : 8 * q + 8]

    def tile(t, carry):
        block = lines[pl.ds(pl.multiple_of(t * DEPTH, 8), DEPTH), :]
        rates[t] = jnp.transpose(block).astype(BF)
        return carry

    lax.fori_loop(0, TILES, tile, 0, unroll=4)


def flat_list(lists, counts, flat):
    me = lax.axis_index("sp")
    ids = lists[...]
    slot = ids - OWN
    offset = (lax.shift_right_arithmetic(slot, 4) - me) & 15
    place = jnp.where(offset < 4, offset - 1, jnp.where(offset == 8, 3, offset - 9))
    ids = jnp.where(slot < 0, ids, OWN + place * CAP + (slot & (CAP - 1))).astype(F32)
    row = jnp.broadcast_to(counts[...], (TILES, TILES))
    sub = lax.broadcasted_iota(I32, (TILES, TILES), 0)
    lane = lax.broadcasted_iota(I32, (TILES, TILES), 1)
    steps_row = lax.shift_right_logical(row + 1, 1)
    count = jnp.sum(jnp.where(lane == sub, row, 0).astype(F32), axis=1, keepdims=True)
    steps = jnp.sum(jnp.where(lane == sub, steps_row, 0).astype(F32), axis=1, keepdims=True)
    base = jnp.sum(jnp.where(lane < sub, steps_row, 0).astype(F32), axis=1, keepdims=True)
    at = lax.broadcasted_iota(I32, (TILES, FLAT), 1).astype(F32)
    tile = lax.broadcasted_iota(I32, (TILES, FLAT), 0).astype(F32)
    hit = jnp.where((at >= base) & (at < base + steps), 1.0, 0.0)
    first = 2.0 * jnp.sum(hit * (at - base), axis=0, keepdims=True)
    which = jnp.sum(hit * tile, axis=0, keepdims=True)
    left = jnp.sum(hit * count, axis=0, keepdims=True)
    total = jnp.sum(steps, axis=0, keepdims=True)
    named = jnp.dot(
        jnp.transpose(ids), hit, preferred_element_type=F32, precision=lax.Precision.HIGHEST
    )
    one = jnp.sum(jnp.where(tile == first, named, 0.0), axis=0, keepdims=True)
    two = jnp.sum(jnp.where(tile == first + 1.0, named, 0.0), axis=0, keepdims=True)
    two = jnp.where(first + 1.0 < left, two, float(DUMMY))
    at = at[0:1]
    one = jnp.where(at < total, one, float(DUMMY))
    word = (which.astype(I32) << 20) | (one.astype(I32) << 10) | two.astype(I32)
    flat[...] = jnp.where(at == float(FLAT - 1), total.astype(I32), word)


def halo_kernel(
    send_ref, coords, weight, lists, counts, centers, width,
    received, feats, rates, weights, flat, pack, lines, send_sem, recv_sem,
):
    me = lax.axis_index("sp")
    greet([sp_peer(o) for o in OFFSETS])
    copies = []
    for p, offset in enumerate(OFFSETS):
        to = lax.rem(me + 16 - offset, 16)
        for k in range(CAP):
            b = send_ref[to, k]
            for c in range(3):
                pack[(p * 4 + c) * CAP + k : (p * 4 + c) * CAP + k + 1, :] = coords[c, pl.ds(b, 1), :]
            pack[(p * 4 + 3) * CAP + k : (p * 4 + 3) * CAP + k + 1, :] = weight[pl.ds(b, 1), :]
        copy = pltpu.make_async_remote_copy(
            src_ref=pack.at[pl.ds(p * 4 * CAP, 4 * CAP)],
            dst_ref=received.at[pl.ds(p * 4 * CAP, 4 * CAP)],
            send_sem=send_sem.at[p],
            recv_sem=recv_sem.at[p],
            device_id=(lax.axis_index("rep"), to),
            device_id_type=MESH,
        )
        copy.start()
        copies.append(copy)

    put_rates(centers, width, rates, lines)
    flat_list(lists, counts, flat)
    weights[0:OWN, :] = weight[...]
    weights[TABLE:ROWS, :] = jnp.zeros((ROWS - TABLE, 128), F32)
    for b in range(TABLE, ROWS):
        feats[b] = jnp.zeros((16, 128), BF)

    def own(i, carry):
        for u in range(4):
            b = pl.multiple_of(32 * i + 8 * u, 8)
            put_features([coords[c, pl.ds(b, 8), :] for c in range(3)], feats, b, lines, u)
        return carry

    lax.fori_loop(0, OWN // 32, own, 0)
    for p, copy in enumerate(copies):
        copy.wait()
        for h in range(CAP // 8):
            rows = [
                received[(p * 4 + c) * CAP + 8 * h : (p * 4 + c) * CAP + 8 * h + 8, :]
                for c in range(4)
            ]
            first = OWN + p * CAP + 8 * h
            put_features(rows[:3], feats, first, lines, (2 * p + h) % 4)
            weights[first : first + 8, :] = rows[3]


def halo(send, coords, weight, lists, counts, centers, width):
    return pl.pallas_call(
        halo_kernel,
        out_shape=(
            jax.ShapeDtypeStruct((4 * HALO, 128), F32),
            jax.ShapeDtypeStruct((ROWS, 16, 128), BF),
            jax.ShapeDtypeStruct((TILES, 128, DEPTH), BF),
            jax.ShapeDtypeStruct((ROWS, 128), F32),
            jax.ShapeDtypeStruct((1, FLAT), I32),
        ),
        in_specs=[SMEM] + [VMEM] * 6,
        out_specs=(VMEM,) * 5,
        scratch_shapes=[
            pltpu.VMEM((4 * HALO, 128), F32),
            pltpu.VMEM((TILES * DEPTH, 128), F32),
            pltpu.SemaphoreType.DMA((len(OFFSETS),)),
            pltpu.SemaphoreType.DMA((len(OFFSETS),)),
        ],
        compiler_params=params(4, 0),
        name="halo",
    )(send, coords, weight, lists, counts, centers, width)


def unpack(word):
    return lax.shift_right_logical(word, 20), lax.shift_right_logical(word, 10) & 1023, word & 1023


def exponents(flat, rates, feats, at):
    t, b1, b2 = unpack(flat[0, at])
    pair = jnp.concatenate([feats[b1], feats[b2]], axis=1)
    ones = jnp.ones((16, 256), BF)
    return jnp.dot(
        rates[t], jnp.concatenate([pair, pair, ones], axis=0), preferred_element_type=F32
    )


def turns_of(count, turns):
    return lax.div(count + (turns - 1), turns)


def model_kernel(turns, depth, flat, rates, feats, weights, model, power, total):
    count = flat[0, FLAT - 1]
    for t in range(TILES):
        total[t] = jnp.zeros((128, 128), F32)

    def add(at, k):
        t, b1, b2 = unpack(flat[0, at])
        total[t] += k[:, :128] * weights[pl.ds(b1, 1), :] + k[:, 128:] * weights[pl.ds(b2, 1), :]

    for d in range(depth):
        power[d] = exponents(flat, rates, feats, d)

    def body(i, carry):
        first = turns * i
        for u in range(turns):
            power[first + u + depth] = exponents(flat, rates, feats, first + u + depth)
            add(first + u, jnp.exp2(power[first + u]))
        return carry

    lax.fori_loop(0, turns_of(jnp.minimum(count, SAVED), turns), body, 0)

    def rest(i, carry):
        for u in range(8):
            at = SAVED + 8 * i + u
            add(at, jnp.exp2(exponents(flat, rates, feats, at)))
        return carry

    lax.fori_loop(0, turns_of(jnp.maximum(count - SAVED, 0), 8), rest, 0)
    for t in range(TILES):
        model[t, :] = jnp.sum(total[t], axis=-1)


def model_pass(flat, rates, feats, weights):
    turns, depth = WORK, 4
    return pl.pallas_call(
        functools.partial(model_kernel, turns, depth),
        out_shape=(
            jax.ShapeDtypeStruct((TILES, 128), F32),
            jax.ShapeDtypeStruct((SAVED + depth, 128, 256), F32),
        ),
        in_specs=[SMEM, VMEM, VMEM, VMEM],
        out_specs=(VMEM, VMEM),
        scratch_shapes=[pltpu.VMEM((TILES, 128, 128), F32)],
        compiler_params=params(4),
        name="model_pass",
    )(flat, rates, feats, weights)


def replica_kernel(
    model, centers, width, density, variance, mean_ref, pull_ref, slots, lines, send_sem, recv_sem
):
    rep, sp = lax.axis_index("rep"), lax.axis_index("sp")
    greet([(lax.rem(rep + d, 8), sp) for d in range(1, 8)])
    copies = []
    for d in range(1, 8):
        copy = pltpu.make_async_remote_copy(
            src_ref=model,
            dst_ref=slots.at[rep],
            send_sem=send_sem.at[d],
            recv_sem=recv_sem.at[d],
            device_id=(lax.rem(rep + d, 8), sp),
            device_id_type=MESH,
        )
        copy.start()
        copies.append(copy)
    slots[rep] = model[...]
    lines[...] = jnp.zeros((TILES * 16, 128), F32)
    for copy in copies:
        copy.wait()
    sum_ = slots[0]
    for r in range(1, 8):
        sum_ = sum_ + slots[r]
    mean = sum_ * 0.125
    mean_ref[...] = mean
    rate = (mean - density[...]) / variance[...] * width[...]
    for row, value in enumerate([rate] + [rate * centers[c] for c in range(3)]):
        hi = value.astype(BF).astype(F32)
        for q in range(TILES // 8):
            lines[pl.ds(128 * q + row, 8, stride=16), :] = hi[8 * q : 8 * q + 8]
            lines[pl.ds(128 * q + 4 + row, 8, stride=16), :] = (value - hi)[8 * q : 8 * q + 8]
    for t in range(TILES):
        rows = lines[16 * t : 16 * t + 16, :].astype(BF)
        pull_ref[t] = jnp.concatenate([rows, rows], axis=1)


def replica_sum(model, centers, width, density, variance):
    return pl.pallas_call(
        replica_kernel,
        out_shape=(
            jax.ShapeDtypeStruct((TILES, 128), F32),
            jax.ShapeDtypeStruct((TILES, 16, 256), BF),
        ),
        in_specs=[VMEM] * 5,
        out_specs=(VMEM, VMEM),
        scratch_shapes=[
            pltpu.VMEM((8, TILES, 128), F32),
            pltpu.VMEM((TILES * 16, 128), F32),
            pltpu.SemaphoreType.DMA((8,)),
            pltpu.SemaphoreType.DMA((8,)),
        ],
        compiler_params=params(4, 1),
        name="replica_sum",
    )(model, centers, width, density, variance)


def force_kernel(
    turns, depth, flat, power, rates, feats, pulls, coords, weights, received,
    own_ref, slot_ref, moments, split,
):
    count = flat[0, FLAT - 1]

    def clear(i, carry):
        moments[pl.ds(pl.multiple_of(128 * i, 128), 128), :] = jnp.zeros((128, 128), F32)
        return carry

    lax.fori_loop(0, ROWS // 16, clear, 0)

    def raise_(value, src):
        k = jnp.exp2(value)
        hi = k.astype(BF)
        split[src, :128] = hi
        split[src, 128:] = (k - hi.astype(F32)).astype(BF)

    def reduce(at, src):
        t, b1, b2 = unpack(flat[0, at])
        both = jnp.dot(pulls[t], split[src], preferred_element_type=F32)
        moments[pl.ds(pl.multiple_of(8 * b1, 8), 8), :] += both[:8, :128]
        moments[pl.ds(pl.multiple_of(8 * b2, 8), 8), :] += both[:8, 128:]

    for d in range(depth):
        raise_(power[d], d)

    def body(i, carry):
        first = turns * i
        for u in range(turns):
            raise_(power[first + u + depth], (u + depth) % RING)
            reduce(first + u, u % RING)
        return carry

    lax.fori_loop(0, turns_of(jnp.minimum(count, SAVED), turns), body, 0)

    def rest(i, carry):
        for u in range(8):
            at = SAVED + 8 * i + u
            raise_(exponents(flat, rates, feats, at), u)
            reduce(at, u)
        return carry

    lax.fori_loop(0, turns_of(jnp.maximum(count - SAVED, 0), 8), rest, 0)

    def summed(first):
        return [
            moments[pl.ds(8 * first + c, 8, stride=8), :]
            + moments[pl.ds(8 * first + 4 + c, 8, stride=8), :]
            for c in range(4)
        ]

    def own(i, carry):
        for u in range(4):
            b = pl.multiple_of(32 * i + 8 * u, 8)
            four = summed(b)
            twice = 2.0 * weights[pl.ds(b, 8), :]
            for c in range(3):
                own_ref[c, pl.ds(b, 8), :] = twice * (coords[c, pl.ds(b, 8), :] * four[0] - four[1 + c])
        return carry

    lax.fori_loop(0, OWN // 32, own, 0)
    for p in range(len(OFFSETS)):
        for h in range(CAP // 8):
            four = summed(OWN + p * CAP + 8 * h)
            at = p * 4 * CAP + 8 * h
            twice = 2.0 * received[at + 3 * CAP : at + 3 * CAP + 8, :]
            for c in range(3):
                xyz = received[at + c * CAP : at + c * CAP + 8, :]
                to = p * BACK + c * CAP + 8 * h
                slot_ref[to : to + 8, :] = twice * (xyz * four[0] - four[1 + c])


def force_pass(flat, power, rates, feats, pulls, coords, weights, received):
    turns, depth = WORK, 2
    return pl.pallas_call(
        functools.partial(force_kernel, turns, depth),
        out_shape=(
            jax.ShapeDtypeStruct((3, OWN, 128), F32),
            jax.ShapeDtypeStruct((3 * HALO, 128), F32),
        ),
        in_specs=[SMEM] + [VMEM] * 7,
        out_specs=(VMEM, VMEM),
        scratch_shapes=[
            pltpu.VMEM((ROWS * 8, 128), F32),
            pltpu.VMEM((RING, 256, 256), BF),
        ],
        compiler_params=params(4),
        name="force_pass",
    )(flat, power, rates, feats, pulls, coords, weights, received)


def return_kernel(slot_ref, out_ref, send_sem, recv_sem):
    greet([sp_peer(o) for o in OFFSETS])
    copies = []
    for p, offset in enumerate(OFFSETS):
        copy = pltpu.make_async_remote_copy(
            src_ref=slot_ref.at[pl.ds(p * BACK, BACK)],
            dst_ref=out_ref.at[pl.ds(p * BACK, BACK)],
            send_sem=send_sem.at[p],
            recv_sem=recv_sem.at[p],
            device_id=sp_peer(offset),
            device_id_type=MESH,
        )
        copy.start()
        copies.append(copy)
    for copy in copies:
        copy.wait()


def return_forces(slots):
    return pl.pallas_call(
        return_kernel,
        out_shape=jax.ShapeDtypeStruct((3 * HALO, 128), F32),
        in_specs=[VMEM],
        out_specs=VMEM,
        scratch_shapes=[
            pltpu.SemaphoreType.DMA((len(OFFSETS),)),
            pltpu.SemaphoreType.DMA((len(OFFSETS),)),
        ],
        compiler_params=params(4, 2),
        name="return_forces",
    )(slots)


def merge_kernel(send_ref, own_ref, back_ref, out_ref):
    out_ref[...] = own_ref[...]
    me = lax.axis_index("sp")
    for p, offset in enumerate(OFFSETS):
        to = lax.rem(me + 16 - offset, 16)
        for k in range(CAP):
            b = send_ref[to, k]
            for c in range(3):
                row = p * BACK + c * CAP + k
                out_ref[c, pl.ds(b, 1), :] += back_ref[row : row + 1, :]


def merge(send, own, back):
    return pl.pallas_call(
        merge_kernel,
        out_shape=jax.ShapeDtypeStruct((3, OWN, 128), F32),
        in_specs=[SMEM, VMEM, VMEM],
        out_specs=VMEM,
        compiler_params=params(4),
        name="merge",
    )(send, own, back)


def local(
    coords, atom_weight, centers, inv_width, density, variance, tile_blocks, tile_counts, send_blocks
):
    own, send = jnp.transpose(coords[0], (1, 0, 2)), send_blocks[0]
    centers = jnp.transpose(centers, (1, 0, 2))
    received, feats, rates, weights, flat = halo(
        send, own, atom_weight, tile_blocks, tile_counts[None], centers, inv_width
    )
    model, power = model_pass(flat, rates, feats, weights)
    mean, pulls = replica_sum(model, centers, inv_width, density, variance)
    forces, slots = force_pass(flat, power, rates, feats, pulls, own, weights, received)
    back = return_forces(slots)
    return jnp.transpose(merge(send, forces, back), (1, 0, 2))[None], mean


def solution(mesh):
    return jax.shard_map(
        local,
        mesh=mesh,
        in_specs=(
            P("rep", "sp", None, None),
            P("sp", None),
            P("sp", None, None),
            P("sp", None),
            P("sp", None),
            P("sp", None),
            P("sp", None),
            P("sp"),
            P("sp", None, None),
        ),
        out_specs=(P("rep", "sp", None, None), P("sp", None)),
        check_vma=False,
    )
```

time: 77.9 us -> 70 us (0.90)
  Pallas kernels: 68.2 us -> 59.9 us
  local copies, waits for them, and re-layouts: 5.44 us -> 8.83 us
  other arithmetic: 3.06 us -> 0 us
    pallas_call x3, Pallas kernels: 27.2 us -> 23.1 us  [the longest x1 11.9 us: halo(): pl.pallas_call(halo_kernel, out_shape=(jax.ShapeDtypeStruct((4 * HALO, 12...]
    unnamed x15 -> x23, local copies, waits for them, and re-layouts: 4.88 us -> 8.83 us
    pallas_call x1, Pallas kernels: 15.7 us -> 12.3 us  [model_pass(): pl.pallas_call(functools.partial(model_kernel, turns, depth), out_shape=(...]
    select_n x3 -> x0, other arithmetic: 1.41 us -> none  [the longest x1 0.68 us: flat_list(): jnp.where(jnp.arange(LIST, dtype=I32)[None, :] < tile_counts[:, None], id...]
    shift_right_arithmetic x1 -> x0, other arithmetic: 1.33 us -> none  [flat_list(): steps = tile_counts + 1 >> 1]
where the time goes in v2:
time: 70 us; the launch traced here: 69.4 us
  Pallas kernels  59.9 us (86%)
  local copies, waits for them, and re-layouts  8.83 us (13%)
  between operations  0.71 us (1%)
    pallas_call x1, Pallas kernels, force_pass(): pl.pallas_call(functools.partial(force_kernel, turns, depth), out_shape=(...  17.5 us
    pallas_call x1, Pallas kernels, model_pass(): pl.pallas_call(functools.partial(model_kernel, turns, depth), out_shape=(...  12.3 us
    pallas_call x1, Pallas kernels, halo(): pl.pallas_call(halo_kernel, out_shape=(jax.ShapeDtypeStruct((4 * HALO, 12...  11.9 us
    pallas_call x1, Pallas kernels, return_forces(): pl.pallas_call(return_kernel, out_shape=jax.ShapeDtypeStruct((3 * HALO, 1...  9.02 us
    unnamed x23, local copies, waits for them, and re-layouts  8.83 us
    pallas_call x1, Pallas kernels, replica_sum(): pl.pallas_call(replica_kernel, out_shape=(jax.ShapeDtypeStruct((TILES, 12...  6.95 us
    pallas_call x1, Pallas kernels, merge(): pl.pallas_call(merge_kernel, out_shape=jax.ShapeDtypeStruct((3, OWN, 128)...  2.14 us

profile of v2, /device:TPU:0, one launch (start us, length us, event | category | flops | bytes accessed | tf_op | source)
XLA Modules:
  0.0 69.4 jit_solution(898286007181309825)
XLA Ops:
  0.6 0.0 copy-start
  0.6 1.1 %copy-done = f32[1,512,3,128]{3,1,2,0:T(8,128)S(1)} copy-done((f32[1,512,3,128]{3,1,2,0:T(8,128)S(1)}, f32[1,512,3,128]{3,1,2,0:T(8,128)}, u32[]{:S(2)}) %copy-start) | copy-done | bytes 786456
  1.8 0.0 copy-start.2
  1.8 0.9 %copy-done.2 = f32[512,128]{1,0:T(8,128)S(1)} copy-done((f32[512,128]{1,0:T(8,128)S(1)}, f32[512,128]{1,0:T(8,128)}, u32[]{:S(2)}) %copy-start.2) | copy-done | bytes 262168
  2.7 0.0 copy-start.3
  2.7 0.8 %copy-done.3 = f32[32,3,128]{2,0,1:T(8,128)S(1)} copy-done((f32[32,3,128]{2,0,1:T(8,128)S(1)}, f32[32,3,128]{2,0,1:T(8,128)}, u32[]{:S(2)}) %copy-start.3) | copy-done | bytes 49176
  3.5 0.0 copy-start.4
  3.5 0.7 %copy-done.4 = f32[32,128]{1,0:T(8,128)S(1)} copy-done((f32[32,128]{1,0:T(8,128)S(1)}, f32[32,128]{1,0:T(8,128)}, u32[]{:S(2)}) %copy-start.4) | copy-done | bytes 16408
  4.2 0.0 copy-start.5
  4.2 0.7 %copy-done.5 = s32[1,16,16]{2,1,0:T(8,128)S(1)} copy-done((s32[1,16,16]{2,1,0:T(8,128)S(1)}, s32[1,16,16]{2,1,0:T(8,128)}, u32[]{:S(2)}) %copy-start.5) | copy-done | bytes 1048
  4.9 0.0 copy-start.7
  4.9 0.7 %copy-done.7 = s32[32,32]{1,0:T(8,128)S(1)} copy-done((s32[32,32]{1,0:T(8,128)S(1)}, s32[32,32]{1,0:T(8,128)}, u32[]{:S(2)}) %copy-start.7) | copy-done | bytes 4120
  5.7 0.0 copy-start.10
  5.7 0.7 copy-done.10
  6.3 0.0 copy-start.6
  6.3 11.9 %halo.1 = (f32[448,128]{1,0:T(8,128)S(1)}, bf16[640,16,128]{2,1,0:T(8,128)(2,1)S(1)}, bf16[32,128,48]{2,1,0:T(8,128)(2,1)S(1)}, f32[640,128]{1,0:T(8,128)S(1)}, s32[1,640]{1,0:T(1,128)S(1)}) custom-call(s32[16,16]{1,0:T(8,128)S(1)} %bitcast.13, f32[3,512,128]{2,1,0:T(8,128)S(1)} %bitcast.9, f32[512,128]{1,0:T(8,128)S(1)} %copy-done.2, ...), custom_call_target="tpu_custom_call" | custom-call | tf_op jit(solution)/shard_map/halo/pallas_call | solution.py:178
  18.2 12.3 %model_pass.1 = (f32[32,128]{1,0:T(8,128)S(1)}, f32[324,128,256]{2,1,0:T(8,128)S(1)}) custom-call(s32[1,640]{1,0:T(1,128)S(1)} %get-tuple-element.13.flat, bf16[32,128,48]{2,1,0:T(8,128)(2,1)S(1)} %get-tuple-element.14.rates, bf16[640,16,128]{2,1,0:T(8,128)(2,1)S(1)} %get-tuple-element.15.feats, f32[640,128]{1,0:T(8,128)S(1)} %get-tuple-element.16.weights), custom_call_target="tpu_custom_call" | custom-call | tf_op jit(solution)/shard_map/model_pass/pallas_call | solution.py:251
  30.6 0.0 copy-start.8
  30.6 0.7 %copy-done.8 = f32[32,128]{1,0:T(8,128)S(1)} copy-done((f32[32,128]{1,0:T(8,128)S(1)}, f32[32,128]{1,0:T(8,128)}, u32[]{:S(2)}) %copy-start.8) | copy-done | bytes 16408
  31.3 0.0 copy-start.9
  31.3 0.7 %copy-done.9 = f32[32,128]{1,0:T(8,128)S(1)} copy-done((f32[32,128]{1,0:T(8,128)S(1)}, f32[32,128]{1,0:T(8,128)}, u32[]{:S(2)}) %copy-start.9) | copy-done | bytes 16408
  32.0 6.9 %replica_sum.1 = (f32[32,128]{1,0:T(8,128)S(1)}, bf16[32,16,256]{2,1,0:T(8,128)(2,1)S(1)}) custom-call(f32[32,128]{1,0:T(8,128)S(1)} %get-tuple-element.18.model, f32[3,32,128]{2,1,0:T(8,128)S(1)} %bitcast.12, f32[32,128]{1,0:T(8,128)S(1)} %copy-done.4, f32[32,128]{1,0:T(8,128)S(1)} %copy-done.8, f32[32,128]{1,0:T(8,128)S(1)} %copy-done.9), custom_call_target="tpu_custom_call" | custom-call | tf_op jit(solution)/shard_map/replica_sum/pallas_call | solution.py:303
  39.0 0.0 copy-start.1
  39.0 1.1 %copy-done.1 = f32[1,512,3,128]{3,1,2,0:T(8,128)S(1)} copy-done((f32[1,512,3,128]{3,1,2,0:T(8,128)S(1)}, f32[1,512,3,128]{3,1,2,0:T(8,128)}, u32[]{:S(2)}) %copy-start.1) | copy-done | bytes 786456
  40.1 17.5 %force_pass.1 = (f32[3,512,128]{2,1,0:T(8,128)S(1)}, f32[336,128]{1,0:T(8,128)S(1)}) custom-call(s32[1,640]{1,0:T(1,128)S(1)} %get-tuple-element.13.flat, f32[324,128,256]{2,1,0:T(8,128)S(1)} %get-tuple-element.17.power, bf16[32,128,48]{2,1,0:T(8,128)(2,1)S(1)} %get-tuple-element.14.rates, bf16[640,16,128]{2,1,0:T(8,128)(2,1)S(1)} %get-tuple-element.15.feats, ...), custom_call_target="tpu_custom_call" | custom-call | tf_op jit(solution)/shard_map/force_pass/pallas_call | solution.py:397
  57.6 9.0 %return_forces.1.back_ref = f32[336,128]{1,0:T(8,128)S(1)} custom-call(f32[336,128]{1,0:T(8,128)S(1)} %get-tuple-element.22.slot_ref), custom_call_target="tpu_custom_call" | custom-call | tf_op jit(solution)/shard_map/return_forces/pallas_call | solution.py:433
  66.7 0.0 copy-done.6
  66.7 2.1 %merge.1 = f32[3,512,128]{2,1,0:T(8,128)} custom-call(s32[16,16]{1,0:T(8,128)S(1)} %bitcast.14, f32[3,512,128]{2,1,0:T(8,128)S(1)} %get-tuple-element.21.own_ref, f32[336,128]{1,0:T(8,128)S(1)} %return_forces.1.back_ref), custom_call_target="tpu_custom_call" | custom-call | tf_op jit(solution)/shard_map/merge/pallas_call | solution.py:460
  68.8 0.6 copy.12
Async XLA Ops:
  0.6 1.1 %copy-start = (f32[1,512,3,128]{3,1,2,0:T(8,128)S(1)}, f32[1,512,3,128]{3,1,2,0:T(8,128)}, u32[]{:S(2)}) copy-start(f32[1,512,3,128]{3,1,2,0:T(8,128)} %param.9) | copy-start | bytes 2359300
  1.8 0.9 %copy-start.2 = (f32[512,128]{1,0:T(8,128)S(1)}, f32[512,128]{1,0:T(8,128)}, u32[]{:S(2)}) copy-start(f32[512,128]{1,0:T(8,128)} %weight.1) | copy-start | bytes 786436
  2.7 0.8 %copy-start.3 = (f32[32,3,128]{2,0,1:T(8,128)S(1)}, f32[32,3,128]{2,0,1:T(8,128)}, u32[]{:S(2)}) copy-start(f32[32,3,128]{2,0,1:T(8,128)} %param.11) | copy-start | bytes 147460
  3.5 0.7 %copy-start.4 = (f32[32,128]{1,0:T(8,128)S(1)}, f32[32,128]{1,0:T(8,128)}, u32[]{:S(2)}) copy-start(f32[32,128]{1,0:T(8,128)} %width.3) | copy-start | bytes 49156
  4.2 0.7 %copy-start.5 = (s32[1,16,16]{2,1,0:T(8,128)S(1)}, s32[1,16,16]{2,1,0:T(8,128)}, u32[]{:S(2)}) copy-start(s32[1,16,16]{2,1,0:T(8,128)} %param.17) | copy-start | bytes 3076
  4.9 0.7 %copy-start.7 = (s32[32,32]{1,0:T(8,128)S(1)}, s32[32,32]{1,0:T(8,128)}, u32[]{:S(2)}) copy-start(s32[32,32]{1,0:T(8,128)} %lists.1) | copy-start | bytes 12292
  5.7 0.7 copy-start.10
  6.3 60.4 %copy-start.6 = (s32[1,16,16]{2,1,0:T(8,128)S(1)}, s32[1,16,16]{2,1,0:T(8,128)}, u32[]{:S(2)}) copy-start(s32[1,16,16]{2,1,0:T(8,128)} %param.17) | copy-start | bytes 3076
  30.6 0.7 %copy-start.8 = (f32[32,128]{1,0:T(8,128)S(1)}, f32[32,128]{1,0:T(8,128)}, u32[]{:S(2)}) copy-start(f32[32,128]{1,0:T(8,128)} %density.1) | copy-start | bytes 49156
  31.3 0.7 %copy-start.9 = (f32[32,128]{1,0:T(8,128)S(1)}, f32[32,128]{1,0:T(8,128)}, u32[]{:S(2)}) copy-start(f32[32,128]{1,0:T(8,128)} %variance.1) | copy-start | bytes 49156
  39.0 1.1 %copy-start.1 = (f32[1,512,3,128]{3,1,2,0:T(8,128)S(1)}, f32[1,512,3,128]{3,1,2,0:T(8,128)}, u32[]{:S(2)}) copy-start(f32[1,512,3,128]{3,1,2,0:T(8,128)} %param.9) | copy-start | bytes 2359300

commit v3 on v2

v3 whole, which is shorter than its diff:
```python
import functools

import jax
import jax.numpy as jnp
from jax import lax
from jax.experimental import pallas as pl
from jax.experimental.pallas import tpu as pltpu
from jax.sharding import PartitionSpec as P

MESH = pl.DeviceIdType.MESH
BF = jnp.bfloat16
F32 = jnp.float32
I32 = jnp.int32
VMEM = pl.BlockSpec(memory_space=pltpu.VMEM)
SMEM = pl.BlockSpec(memory_space=pltpu.SMEM)
HBM = pl.BlockSpec(memory_space=pltpu.HBM)

OFFSETS = (1, 2, 3, 8, 13, 14, 15)
CAP = 16
OWN = 512
HALO = len(OFFSETS) * CAP
TABLE = OWN + HALO
DUMMY = TABLE
ROWS = TABLE + CAP
TILES = 32
LIST = 32
STEPS = TILES * LIST // 2
FLAT = 640
SURE = 10
FIXED = TILES * SURE
BACK = 3 * CAP
DEPTH = 48
RING = 8
GROUPS = 4
LOG2E = 1.4426950408889634


def params(limit_mib, collective_id=None):
    more = {} if collective_id is None else {"collective_id": collective_id, "has_side_effects": True}
    return pltpu.CompilerParams(vmem_limit_bytes=limit_mib << 20, **more)


def sp_peer(offset):
    return (lax.axis_index("rep"), lax.rem(lax.axis_index("sp") + offset, 16))


def greet(peers):
    barrier = pltpu.get_barrier_semaphore()
    for peer in peers:
        pl.semaphore_signal(barrier, inc=1, device_id=peer, device_id_type=MESH)
    pl.semaphore_wait(barrier, len(peers))


def pieces(x):
    hi = x.astype(BF).astype(F32)
    rest = x - hi
    mid = rest.astype(BF).astype(F32)
    return hi, mid, rest - mid


def put_features(xyz, feats, first, lines, at):
    square = xyz[0] * xyz[0] + xyz[1] * xyz[1] + xyz[2] * xyz[2]
    for row, value in enumerate((*xyz, square)):
        hi, mid, lo = pieces(value)
        for group, piece in enumerate((hi, mid, hi, lo)):
            lines[pl.ds(at * 128 + 4 * group + row, 8, stride=16), :] = piece
    for b in range(8):
        feats[first + b] = lines[at * 128 + 16 * b : at * 128 + 16 * b + 16, :].astype(BF)


def put_rates(centers, width, rates, lines):
    slope = width[...] * LOG2E
    x = [centers[c] for c in range(3)]
    size = x[0] * x[0] + x[1] * x[1] + x[2] * x[2]
    zero = jnp.zeros((TILES, 128), F32)
    rows = [zero] * DEPTH
    for c, value in enumerate([2.0 * slope * x[0], 2.0 * slope * x[1], 2.0 * slope * x[2], -slope]):
        hi, mid, lo = pieces(value)
        for group, piece in enumerate((hi, hi, mid, hi, lo, mid)):
            rows[4 * group + c] = piece
    for at, piece in enumerate(pieces(-slope * size)):
        rows[32 + at] = piece
    for r in range(DEPTH):
        for q in range(TILES // 8):
            lines[pl.ds(8 * q * DEPTH + r, 8, stride=DEPTH), :] = rows[r][8 * q : 8 * q + 8]

    def tile(t, carry):
        block = lines[pl.ds(pl.multiple_of(t * DEPTH, 8), DEPTH), :]
        rates[t] = jnp.transpose(block).astype(BF)
        return carry

    lax.fori_loop(0, TILES, tile, 0, unroll=4)


def flat_list(lists, counts, flat):
    me = lax.axis_index("sp")
    ids = lists[...]
    slot = ids - OWN
    offset = (lax.shift_right_arithmetic(slot, 4) - me) & 15
    place = jnp.where(offset < 4, offset - 1, jnp.where(offset == 8, 3, offset - 9))
    ids = jnp.where(slot < 0, ids, OWN + place * CAP + (slot & (CAP - 1))).astype(F32)
    row = jnp.broadcast_to(counts[...], (TILES, TILES))
    sub = lax.broadcasted_iota(I32, (TILES, TILES), 0)
    lane = lax.broadcasted_iota(I32, (TILES, TILES), 1)
    more_row = (lax.shift_right_logical(row + 1, 1) - SURE).astype(F32)
    count = jnp.sum(jnp.where(lane == sub, row.astype(F32), 0.0), axis=1, keepdims=True)
    more = jnp.sum(jnp.where(lane == sub, more_row, 0.0), axis=1, keepdims=True)
    base = jnp.sum(jnp.where(lane < sub, more_row, 0.0), axis=1, keepdims=True) + float(FIXED)
    at = lax.broadcasted_iota(I32, (TILES, FLAT), 1).astype(F32)
    tile = lax.broadcasted_iota(I32, (TILES, FLAT), 0).astype(F32)
    sure = (at >= SURE * tile) & (at < SURE * tile + SURE)
    hit = jnp.where(sure | ((at >= base) & (at < base + more)), 1.0, 0.0)
    step = jnp.where(sure, at - SURE * tile, at - base + SURE)
    first = 2.0 * jnp.sum(hit * step, axis=0, keepdims=True)
    which = jnp.sum(hit * tile, axis=0, keepdims=True)
    left = jnp.sum(hit * count, axis=0, keepdims=True)
    total = jnp.sum(more, axis=0, keepdims=True)
    named = jnp.dot(
        jnp.transpose(ids), hit, preferred_element_type=F32, precision=lax.Precision.HIGHEST
    )
    one = jnp.sum(jnp.where(tile == first, named, 0.0), axis=0, keepdims=True)
    two = jnp.sum(jnp.where(tile == first + 1.0, named, 0.0), axis=0, keepdims=True)
    two = jnp.where(first + 1.0 < left, two, float(DUMMY))
    at = at[0:1]
    one = jnp.where(at < total + float(FIXED), one, float(DUMMY))
    word = (which.astype(I32) << 20) | (one.astype(I32) << 10) | two.astype(I32)
    flat[...] = jnp.where(at == float(FLAT - 1), total.astype(I32), word)


def halo_kernel(
    send_hbm, coords_hbm, weight_hbm, lists_hbm, counts_hbm, centers_hbm, width_hbm, density_hbm, variance_hbm,
    received, feats, rates, weights, flat, coords, centers, width, density, variance,
    pack, lines, lists, counts, send_ref, near_sem, send_sem, recv_sem,
):
    me = lax.axis_index("sp")
    barrier = pltpu.get_barrier_semaphore()
    for offset in OFFSETS:
        pl.semaphore_signal(barrier, inc=1, device_id=sp_peer(offset), device_id_type=MESH)
    near = [
        pltpu.make_async_copy(src, dst, near_sem.at[i])
        for i, (src, dst) in enumerate((
            (send_hbm, send_ref),
            (coords_hbm, coords),
            (weight_hbm, weights.at[pl.ds(0, OWN)]),
            (centers_hbm, centers),
            (width_hbm, width),
            (lists_hbm, lists),
            (counts_hbm, counts),
            (density_hbm, density),
            (variance_hbm, variance),
        ))
    ]
    for copy in near:
        copy.start()
    for copy in near[:3]:
        copy.wait()

    def gather(p):
        to = lax.rem(me + 16 - OFFSETS[p], 16)
        for k in range(CAP):
            b = send_ref[to, k]
            for c in range(3):
                pack[(p * 4 + c) * CAP + k : (p * 4 + c) * CAP + k + 1, :] = coords[c, pl.ds(b, 1), :]
            pack[(p * 4 + 3) * CAP + k : (p * 4 + 3) * CAP + k + 1, :] = weights[pl.ds(b, 1), :]

    copies = []
    for p, offset in enumerate(OFFSETS):
        gather(p)
        if p == 0:
            pl.semaphore_wait(barrier, len(OFFSETS))
        copy = pltpu.make_async_remote_copy(
            src_ref=pack.at[pl.ds(p * 4 * CAP, 4 * CAP)],
            dst_ref=received.at[pl.ds(p * 4 * CAP, 4 * CAP)],
            send_sem=send_sem.at[p],
            recv_sem=recv_sem.at[p],
            device_id=sp_peer(16 - offset),
            device_id_type=MESH,
        )
        copy.start()
        copies.append(copy)

    for copy in near[3:]:
        copy.wait()
    put_rates(centers, width, rates, lines)
    flat_list(lists, counts, flat)
    weights[TABLE:ROWS, :] = jnp.zeros((ROWS - TABLE, 128), F32)
    for b in range(TABLE, ROWS):
        feats[b] = jnp.zeros((16, 128), BF)

    def own(i, carry):
        for u in range(4):
            b = pl.multiple_of(32 * i + 8 * u, 8)
            put_features([coords[c, pl.ds(b, 8), :] for c in range(3)], feats, b, lines, u)
        return carry

    lax.fori_loop(0, OWN // 32, own, 0)
    for p, copy in enumerate(copies):
        copy.wait()
        for h in range(CAP // 8):
            rows = [
                received[(p * 4 + c) * CAP + 8 * h : (p * 4 + c) * CAP + 8 * h + 8, :]
                for c in range(4)
            ]
            first = OWN + p * CAP + 8 * h
            put_features(rows[:3], feats, first, lines, (2 * p + h) % 4)
            weights[first : first + 8, :] = rows[3]


def halo(send, coords, weight, lists, counts, centers, width, density, variance):
    small = jax.ShapeDtypeStruct((TILES, 128), F32)
    return pl.pallas_call(
        halo_kernel,
        out_shape=(
            jax.ShapeDtypeStruct((4 * HALO, 128), F32),
            jax.ShapeDtypeStruct((ROWS, 16, 128), BF),
            jax.ShapeDtypeStruct((TILES, 128, DEPTH), BF),
            jax.ShapeDtypeStruct((ROWS, 128), F32),
            jax.ShapeDtypeStruct((1, FLAT), I32),
            jax.ShapeDtypeStruct((3, OWN, 128), F32),
            jax.ShapeDtypeStruct((3, TILES, 128), F32),
            small,
            small,
            small,
        ),
        in_specs=[HBM] * 9,
        out_specs=(VMEM,) * 10,
        scratch_shapes=[
            pltpu.VMEM((4 * HALO, 128), F32),
            pltpu.VMEM((TILES * DEPTH, 128), F32),
            pltpu.VMEM((TILES, LIST), I32),
            pltpu.VMEM((1, TILES), I32),
            pltpu.SMEM((16, CAP), I32),
            pltpu.SemaphoreType.DMA((9,)),
            pltpu.SemaphoreType.DMA((len(OFFSETS),)),
            pltpu.SemaphoreType.DMA((len(OFFSETS),)),
        ],
        compiler_params=params(4, 0),
        name="halo",
    )(send, coords, weight, lists, counts, centers, width, density, variance)


def unpack(word):
    return lax.shift_right_logical(word, 20), lax.shift_right_logical(word, 10) & 1023, word & 1023


def exponents(flat, rates, feats, at):
    t, b1, b2 = unpack(flat[0, at])
    pair = jnp.concatenate([feats[b1], feats[b2]], axis=1)
    ones = jnp.ones((16, 256), BF)
    return jnp.dot(
        rates[t], jnp.concatenate([pair, pair, ones], axis=0), preferred_element_type=F32
    )


def turns_of(count, turns):
    return lax.div(count + (turns - 1), turns)


def weighed(flat, weights, at, k):
    t, b1, b2 = unpack(flat[0, at])
    return t, k[:, :128] * weights[pl.ds(b1, 1), :] + k[:, 128:] * weights[pl.ds(b2, 1), :]


def rest_kernel(turns, depth, flat, rates, feats, weights, total, power):
    count = flat[0, FLAT - 1]
    for t in range(TILES):
        total[t] = jnp.zeros((128, 128), F32)
    for d in range(depth):
        power[d] = exponents(flat, rates, feats, FIXED + d)

    def body(i, carry):
        first = FIXED + turns * i
        for u in range(turns):
            power[(u + depth) % turns] = exponents(flat, rates, feats, first + u + depth)
            t, more = weighed(flat, weights, first + u, jnp.exp2(power[u]))
            total[t] += more
        return carry

    lax.fori_loop(0, turns_of(count, turns), body, 0)


def rest_pass(flat, rates, feats, weights):
    turns, depth = 16, 4
    return pl.pallas_call(
        functools.partial(rest_kernel, turns, depth),
        out_shape=jax.ShapeDtypeStruct((TILES, 128, 128), F32),
        in_specs=[SMEM, VMEM, VMEM, VMEM],
        out_specs=VMEM,
        scratch_shapes=[pltpu.VMEM((turns, 128, 256), F32)],
        compiler_params=params(4),
        name="rest_pass",
    )(flat, rates, feats, weights)


def raise_(value, split, src):
    k = jnp.exp2(value)
    hi = k.astype(BF)
    split[src, :128] = hi
    split[src, 128:] = (k - hi.astype(F32)).astype(BF)


def main_kernel(
    bunch, ahead, flat, rates, feats, weights, begun, centers, width, density, variance,
    mean_ref, pull_ref, both_ref, power, split, total, model, slots, lines, send_sem, recv_sem,
):
    rep, sp = lax.axis_index("rep"), lax.axis_index("sp")
    peers = [(lax.rem(rep + d, 8), sp) for d in range(1, 8)]
    barrier = pltpu.get_barrier_semaphore()
    for peer in peers:
        pl.semaphore_signal(barrier, inc=1, device_id=peer, device_id_type=MESH)
    per_group = TILES // GROUPS
    turns = bunch * SURE
    for d in range(ahead):
        power[d] = exponents(flat, rates, feats, d)

    def send(group):
        rows = pl.ds(pl.multiple_of(per_group * group, 8), per_group)
        return [
            pltpu.make_async_remote_copy(
                src_ref=model.at[rows],
                dst_ref=slots.at[rep, rows],
                send_sem=send_sem.at[group, d],
                recv_sem=recv_sem.at[group, d],
                device_id=peer,
                device_id_type=MESH,
            )
            for d, peer in enumerate(peers)
        ]

    def first_pass(group, carry):
        def body(i, carry):
            tile = per_group * group + bunch * i
            first = tile * SURE
            for u in range(turns):
                power[first + u + ahead] = exponents(flat, rates, feats, first + u + ahead)
                own_tile = u // SURE
                unused_t, more = weighed(flat, weights, first + u, jnp.exp2(power[first + u]))
                if u % SURE == 0:
                    total[own_tile] = begun[tile + own_tile] + more
                else:
                    total[own_tile] += more
            for j in range(bunch):
                model[pl.ds(tile + j, 1), :] = jnp.sum(total[j], axis=-1)[None, :]
            return carry

        lax.fori_loop(0, per_group // bunch, body, 0)

        @pl.when(group == 0)
        def _():
            pl.semaphore_wait(barrier, 7)

        for copy in send(group):
            copy.start()
        return carry

    lax.fori_loop(0, GROUPS, first_pass, 0)
    lines[...] = jnp.zeros((per_group * 16, 128), F32)
    for d in range(2):
        raise_(power[d], split, d)

    def second_pass(group, carry):
        rows = pl.ds(pl.multiple_of(per_group * group, 8), per_group)
        slots[rep, rows] = model[rows, :]
        for copy in send(group):
            copy.wait()
        sum_ = slots[0, rows]
        for r in range(1, 8):
            sum_ = sum_ + slots[r, rows]
        mean = sum_ * 0.125
        mean_ref[rows, :] = mean
        rate = (mean - density[rows, :]) / variance[rows, :] * width[rows, :]
        for row, value in enumerate([rate] + [rate * centers[c, rows] for c in range(3)]):
            hi = value.astype(BF).astype(F32)
            lines[pl.ds(row, 8, stride=16), :] = hi
            lines[pl.ds(4 + row, 8, stride=16), :] = value - hi
        for j in range(per_group):
            eight = lines[16 * j : 16 * j + 16, :].astype(BF)
            pull_ref[per_group * group + j] = jnp.concatenate([eight, eight], axis=1)

        def body(i, carry):
            tile = per_group * group + bunch * i
            first = tile * SURE
            for u in range(turns):
                raise_(power[first + u + 2], split, (u + 2) % RING)
                both_ref[first + u] = jnp.dot(
                    pull_ref[tile + u // SURE], split[u % RING], preferred_element_type=F32
                )[:8]
            return carry

        lax.fori_loop(0, per_group // bunch, body, 0)
        return carry

    lax.fori_loop(0, GROUPS, second_pass, 0)


def main_pass(flat, rates, feats, weights, begun, centers, width, density, variance):
    bunch, ahead = 4, 4
    return pl.pallas_call(
        functools.partial(main_kernel, bunch, ahead),
        out_shape=(
            jax.ShapeDtypeStruct((TILES, 128), F32),
            jax.ShapeDtypeStruct((TILES, 16, 256), BF),
            jax.ShapeDtypeStruct((FIXED, 8, 256), F32),
        ),
        in_specs=[SMEM] + [VMEM] * 8,
        out_specs=(VMEM, VMEM, VMEM),
        scratch_shapes=[
            pltpu.VMEM((FIXED + ahead, 128, 256), F32),
            pltpu.VMEM((RING, 256, 256), BF),
            pltpu.VMEM((bunch, 128, 128), F32),
            pltpu.VMEM((TILES, 128), F32),
            pltpu.VMEM((8, TILES, 128), F32),
            pltpu.VMEM((TILES // GROUPS * 16, 128), F32),
            pltpu.SemaphoreType.DMA((GROUPS, 7)),
            pltpu.SemaphoreType.DMA((GROUPS, 7)),
        ],
        compiler_params=params(44, 1),
        name="main_pass",
    )(flat, rates, feats, weights, begun, centers, width, density, variance)


def summed(moments, first):
    return [
        moments[pl.ds(8 * first + c, 8, stride=8), :]
        + moments[pl.ds(8 * first + 4 + c, 8, stride=8), :]
        for c in range(4)
    ]


def force_kernel(turns, flat, rates, feats, pulls, both_ref, received, slot_ref, moments, power, split):
    count = flat[0, FLAT - 1]

    def clear(i, carry):
        moments[pl.ds(pl.multiple_of(128 * i, 128), 128), :] = jnp.zeros((128, 128), F32)
        return carry

    lax.fori_loop(0, ROWS // 16, clear, 0)

    def put(at, both):
        unused_t, b1, b2 = unpack(flat[0, at])
        moments[pl.ds(pl.multiple_of(8 * b1, 8), 8), :] += both[:8, :128]
        moments[pl.ds(pl.multiple_of(8 * b2, 8), 8), :] += both[:8, 128:]

    def known(i, carry):
        for u in range(8):
            put(8 * i + u, both_ref[8 * i + u])
        return carry

    lax.fori_loop(0, FIXED // 8, known, 0)
    for d in range(4):
        power[d] = exponents(flat, rates, feats, FIXED + d)
    for d in range(2):
        raise_(power[d], split, d)

    def body(i, carry):
        first = FIXED + turns * i
        for u in range(turns):
            power[(u + 4) % turns] = exponents(flat, rates, feats, first + u + 4)
            raise_(power[(u + 2) % turns], split, (u + 2) % turns)
            t = lax.shift_right_logical(flat[0, first + u], 20)
            put(first + u, jnp.dot(pulls[t], split[u % turns], preferred_element_type=F32))
        return carry

    lax.fori_loop(0, turns_of(count, turns), body, 0)
    for p in range(len(OFFSETS)):
        for h in range(CAP // 8):
            four = summed(moments, OWN + p * CAP + 8 * h)
            at = p * 4 * CAP + 8 * h
            twice = 2.0 * received[at + 3 * CAP : at + 3 * CAP + 8, :]
            for c in range(3):
                xyz = received[at + c * CAP : at + c * CAP + 8, :]
                to = p * BACK + c * CAP + 8 * h
                slot_ref[to : to + 8, :] = twice * (xyz * four[0] - four[1 + c])


def force_pass(flat, rates, feats, pulls, both, received):
    turns = 16
    return pl.pallas_call(
        functools.partial(force_kernel, turns),
        out_shape=(
            jax.ShapeDtypeStruct((3 * HALO, 128), F32),
            jax.ShapeDtypeStruct((ROWS * 8, 128), F32),
        ),
        in_specs=[SMEM] + [VMEM] * 5,
        out_specs=(VMEM, VMEM),
        scratch_shapes=[
            pltpu.VMEM((turns, 128, 256), F32),
            pltpu.VMEM((turns, 256, 256), BF),
        ],
        compiler_params=params(6),
        name="force_pass",
    )(flat, rates, feats, pulls, both, received)


def return_kernel(slot_ref, moments, coords, weights, out_ref, own_ref, send_sem, recv_sem):
    greet([sp_peer(o) for o in OFFSETS])
    copies = []
    for p, offset in enumerate(OFFSETS):
        copy = pltpu.make_async_remote_copy(
            src_ref=slot_ref.at[pl.ds(p * BACK, BACK)],
            dst_ref=out_ref.at[pl.ds(p * BACK, BACK)],
            send_sem=send_sem.at[p],
            recv_sem=recv_sem.at[p],
            device_id=sp_peer(offset),
            device_id_type=MESH,
        )
        copy.start()
        copies.append(copy)

    def own(i, carry):
        for u in range(4):
            b = pl.multiple_of(32 * i + 8 * u, 8)
            four = summed(moments, b)
            twice = 2.0 * weights[pl.ds(b, 8), :]
            for c in range(3):
                own_ref[c, pl.ds(b, 8), :] = twice * (coords[c, pl.ds(b, 8), :] * four[0] - four[1 + c])
        return carry

    lax.fori_loop(0, OWN // 32, own, 0)
    for copy in copies:
        copy.wait()


def return_forces(slots, moments, coords, weights):
    return pl.pallas_call(
        return_kernel,
        out_shape=(
            jax.ShapeDtypeStruct((3 * HALO, 128), F32),
            jax.ShapeDtypeStruct((3, OWN, 128), F32),
        ),
        in_specs=[VMEM] * 4,
        out_specs=(VMEM, VMEM),
        scratch_shapes=[
            pltpu.SemaphoreType.DMA((len(OFFSETS),)),
            pltpu.SemaphoreType.DMA((len(OFFSETS),)),
        ],
        compiler_params=params(4, 2),
        name="return_forces",
    )(slots, moments, coords, weights)


def merge_kernel(send_ref, own_ref, back_ref, out_ref):
    out_ref[...] = own_ref[...]
    me = lax.axis_index("sp")
    for p, offset in enumerate(OFFSETS):
        to = lax.rem(me + 16 - offset, 16)
        for k in range(CAP):
            b = send_ref[to, k]
            for c in range(3):
                row = p * BACK + c * CAP + k
                out_ref[c, pl.ds(b, 1), :] += back_ref[row : row + 1, :]


def merge(send, own, back):
    return pl.pallas_call(
        merge_kernel,
        out_shape=jax.ShapeDtypeStruct((3, OWN, 128), F32),
        in_specs=[SMEM, VMEM, VMEM],
        out_specs=VMEM,
        compiler_params=params(4),
        name="merge",
    )(send, own, back)


def local(
    coords, atom_weight, centers, inv_width, density, variance, tile_blocks, tile_counts, send_blocks
):
    own, send = jnp.transpose(coords[0], (1, 0, 2)), send_blocks[0]
    centers = jnp.transpose(centers, (1, 0, 2))
    given = (send, own, atom_weight, tile_blocks, tile_counts[None], centers, inv_width, density, variance)
    received, feats, rates, weights, flat, own, centers, width, density, variance = halo(
        *[pltpu.with_memory_space_constraint(x, pltpu.HBM) for x in given]
    )
    begun = rest_pass(flat, rates, feats, weights)
    mean, pulls, both = main_pass(
        flat, rates, feats, weights, begun, centers, width, density, variance
    )
    slots, moments = force_pass(flat, rates, feats, pulls, both, received)
    back, forces = return_forces(slots, moments, own, weights)
    return jnp.transpose(merge(send, forces, back), (1, 0, 2))[None], mean


def solution(mesh):
    return jax.shard_map(
        local,
        mesh=mesh,
        in_specs=(
            P("rep", "sp", None, None),
            P("sp", None),
            P("sp", None, None),
            P("sp", None),
            P("sp", None),
            P("sp", None),
            P("sp", None),
            P("sp"),
            P("sp", None, None),
        ),
        out_specs=(P("rep", "sp", None, None), P("sp", None)),
        check_vma=False,
    )
```

time: 70 us -> 55.7 us (0.80)
  local copies, waits for them, and re-layouts: 8.83 us -> 0.61 us
  Pallas kernels: 59.9 us -> 54.3 us
    unnamed x23 -> x3, local copies, waits for them, and re-layouts: 8.83 us -> 0.61 us
    pallas_call x4, Pallas kernels: 45.8 us -> 40.6 us  [the longest x1 20.2 us: main_pass(): pl.pallas_call(functools.partial(main_kernel, bunch, ahead), out_shape=(j...]
where the time goes in v3:
time: 55.7 us; the launch traced here: 55.6 us
  Pallas kernels  54.3 us (97%)
  between operations  0.69 us (1%)
  local copies, waits for them, and re-layouts  0.61 us (1%)
    pallas_call x1, Pallas kernels, main_pass(): pl.pallas_call(functools.partial(main_kernel, bunch, ahead), out_shape=(j...  20.2 us
    pallas_call x1, Pallas kernels, halo(): pl.pallas_call(halo_kernel, out_shape=(jax.ShapeDtypeStruct((4 * HALO, 12...  11.5 us
    pallas_call x1, Pallas kernels, return_forces(): pl.pallas_call(return_kernel, out_shape=(jax.ShapeDtypeStruct((3 * HALO,...  9.29 us
    pallas_call x1, Pallas kernels, force_pass(): pl.pallas_call(functools.partial(force_kernel, turns), out_shape=(jax.Sha...  7.77 us
    pallas_call x1, Pallas kernels, rest_pass(): pl.pallas_call(functools.partial(rest_kernel, turns, depth), out_shape=ja...  3.37 us
    pallas_call x1, Pallas kernels, merge(): pl.pallas_call(merge_kernel, out_shape=jax.ShapeDtypeStruct((3, OWN, 128)...  2.14 us

profile of v3, /device:TPU:0, one launch (start us, length us, event | category | flops | bytes accessed | tf_op | source)
XLA Modules:
  0.0 55.6 jit_solution(8447118906879214579)
XLA Ops:
  0.6 11.5 %halo.1 = (f32[448,128]{1,0:T(8,128)S(1)}, bf16[640,16,128]{2,1,0:T(8,128)(2,1)S(1)}, bf16[32,128,48]{2,1,0:T(8,128)(2,1)S(1)}, f32[640,128]{1,0:T(8,128)S(1)}, ...) custom-call(s32[16,16]{1,0:T(8,128)} %bitcast.9, ...), custom_call_target="tpu_custom_call" | custom-call | tf_op jit(solution)/shard_map/halo/pallas_call | solution.py:211
  12.2 3.4 %rest_pass.1.begun = f32[32,128,128]{2,1,0:T(8,128)S(1)} custom-call(s32[1,640]{1,0:T(1,128)S(1)} %get-tuple-element.19.flat, bf16[32,128,48]{2,1,0:T(8,128)(2,1)S(1)} %get-tuple-element.20.rates, bf16[640,16,128]{2,1,0:T(8,128)(2,1)S(1)} %get-tuple-element.21.feats, f32[640,128]{1,0:T(8,128)S(1)} %get-tuple-element.22.weights), custom_call_target="tpu_custom_call" | custom-call | tf_op jit(solution)/shard_map/rest_pass/pallas_call | solution.py:284
  15.5 20.2 %main_pass.1 = (f32[32,128]{1,0:T(8,128)S(1)}, bf16[32,16,256]{2,1,0:T(8,128)(2,1)S(1)}, f32[320,8,256]{2,1,0:T(8,128)S(1)}) custom-call(s32[1,640]{1,0:T(1,128)S(1)} %get-tuple-element.19.flat, bf16[32,128,48]{2,1,0:T(8,128)(2,1)S(1)} %get-tuple-element.20.rates, bf16[640,16,128]{2,1,0:T(8,128)(2,1)S(1)} %get-tuple-element.21.feats, ...), custom_call_target="tpu_custom_call" | custom-call | tf_op jit(solution)/shard_map/main_pass/pallas_call | solution.py:398
  35.7 7.8 %force_pass.1 = (f32[336,128]{1,0:T(8,128)S(1)}, f32[5120,128]{1,0:T(8,128)S(1)}) custom-call(s32[1,640]{1,0:T(1,128)S(1)} %get-tuple-element.19.flat, bf16[32,128,48]{2,1,0:T(8,128)(2,1)S(1)} %get-tuple-element.20.rates, bf16[640,16,128]{2,1,0:T(8,128)(2,1)S(1)} %get-tuple-element.21.feats, bf16[32,16,256]{2,1,0:T(8,128)(2,1)S(1)} %get-tuple-element.27.pulls, ...), custom_call_target="tpu_custom_call" | custom-call | tf_op jit(solution)/shard_map/force_pass/pallas_call | solution.py:478
  43.5 0.0 copy-start
  43.5 9.3 %return_forces.1 = (f32[336,128]{1,0:T(8,128)S(1)}, f32[3,512,128]{2,1,0:T(8,128)S(1)}) custom-call(f32[336,128]{1,0:T(8,128)S(1)} %get-tuple-element.30.slot_ref, f32[5120,128]{1,0:T(8,128)S(1)} %get-tuple-element.31.moments, f32[3,512,128]{2,1,0:T(8,128)S(1)} %get-tuple-element.32.coords, f32[640,128]{1,0:T(8,128)S(1)} %get-tuple-element.22.weights), custom_call_target="tpu_custom_call" | custom-call | tf_op jit(solution)/shard_map/return_forces/pallas_call | solution.py:525
  52.8 0.0 copy-done
  52.8 2.1 %merge.1 = f32[3,512,128]{2,1,0:T(8,128)} custom-call(s32[16,16]{1,0:T(8,128)S(1)} %bitcast.10, f32[3,512,128]{2,1,0:T(8,128)S(1)} %get-tuple-element.33.own_ref, f32[336,128]{1,0:T(8,128)S(1)} %get-tuple-element.34.back_ref), custom_call_target="tpu_custom_call" | custom-call | tf_op jit(solution)/shard_map/merge/pallas_call | solution.py:555
  55.0 0.6 %copy.12 = f32[32,128]{1,0:T(8,128)} copy(f32[32,128]{1,0:T(8,128)S(1)} %get-tuple-element.39) | data formatting | bytes 32768
Async XLA Ops:
  43.5 9.3 %copy-start = (s32[1,16,16]{2,1,0:T(8,128)S(1)}, s32[1,16,16]{2,1,0:T(8,128)}, u32[]{:S(2)}) copy-start(s32[1,16,16]{2,1,0:T(8,128)} %param.17) | copy-start | bytes 3076

commit v4 on v0

v4 whole, which is shorter than its diff:
```python
import functools

import jax
import jax.numpy as jnp
from jax import lax
from jax.experimental import pallas as pl
from jax.experimental.pallas import tpu as pltpu
from jax.sharding import PartitionSpec as P

MESH = pl.DeviceIdType.MESH
BF = jnp.bfloat16
F32 = jnp.float32
I32 = jnp.int32
VMEM = pl.BlockSpec(memory_space=pltpu.VMEM)
SMEM = pl.BlockSpec(memory_space=pltpu.SMEM)
HBM = pl.BlockSpec(memory_space=pltpu.HBM)

OFFSETS = (1, 2, 3, 8, 13, 14, 15)
CAP = 16
OWN = 512
HALO = len(OFFSETS) * CAP
TABLE = OWN + HALO
DUMMY = TABLE
ROWS = TABLE + CAP
TILES = 32
LIST = 32
STEPS = TILES * LIST // 2
GROUPS = 4
TILES_OF = TILES // GROUPS
STEPS_OF = STEPS // GROUPS
PAIRS_OF = TILES_OF * LIST
BUNCH = 4
BACK = 3 * CAP
DEPTH = 48
LOG2E = 1.4426950408889634


def params(limit_mib, collective_id=None):
    more = {} if collective_id is None else {"collective_id": collective_id, "has_side_effects": True}
    return pltpu.CompilerParams(vmem_limit_bytes=limit_mib << 20, **more)


def sp_peer(offset):
    return (lax.axis_index("rep"), lax.rem(lax.axis_index("sp") + offset, 16))


def pieces(x):
    hi = x.astype(BF).astype(F32)
    rest = x - hi
    mid = rest.astype(BF).astype(F32)
    return hi, mid, rest - mid


def put_features(xyz, feats, first, lines, at):
    square = xyz[0] * xyz[0] + xyz[1] * xyz[1] + xyz[2] * xyz[2]
    for row, value in enumerate((*xyz, square)):
        hi, mid, lo = pieces(value)
        for group, piece in enumerate((hi, mid, hi, lo)):
            lines[pl.ds(at * 128 + 4 * group + row, 8, stride=16), :] = piece
    for b in range(8):
        feats[first + b] = lines[at * 128 + 16 * b : at * 128 + 16 * b + 16, :].astype(BF)


def put_rates(centers, width, rates, lines):
    slope = width[...] * LOG2E
    x = [centers[c] for c in range(3)]
    size = x[0] * x[0] + x[1] * x[1] + x[2] * x[2]
    zero = jnp.zeros((TILES, 128), F32)
    rows = [zero] * DEPTH
    for c, value in enumerate([2.0 * slope * x[0], 2.0 * slope * x[1], 2.0 * slope * x[2], -slope]):
        hi, mid, lo = pieces(value)
        for group, piece in enumerate((hi, hi, mid, hi, lo, mid)):
            rows[4 * group + c] = piece
    for at, piece in enumerate(pieces(-slope * size)):
        rows[32 + at] = piece
    for r in range(DEPTH):
        for q in range(TILES // 8):
            lines[pl.ds(8 * q * DEPTH + r, 8, stride=DEPTH), :] = rows[r][8 * q : 8 * q + 8]

    def tile(t, carry):
        block = lines[pl.ds(pl.multiple_of(t * DEPTH, 8), DEPTH), :]
        rates[t] = jnp.transpose(block).astype(BF)
        return carry

    lax.fori_loop(0, TILES, tile, 0, unroll=4)


def table_ids(lists, counts, ids):
    me = lax.axis_index("sp")
    named = lists[...]
    slot = named - OWN
    offset = (lax.shift_right_arithmetic(slot, 4) - me) & 15
    place = jnp.where(offset < 4, offset - 1, jnp.where(offset == 8, 3, offset - 9))
    named = jnp.where(slot < 0, named, OWN + place * CAP + (slot & (CAP - 1)))
    row = jnp.broadcast_to(counts[...], (TILES, TILES)).astype(F32)
    sub = lax.broadcasted_iota(I32, (TILES, TILES), 0)
    lane = lax.broadcasted_iota(I32, (TILES, TILES), 1)
    count = jnp.sum(jnp.where(lane == sub, row, 0.0), axis=1, keepdims=True)
    ids[...] = jnp.where(lane.astype(F32) < count, named, DUMMY)


def two_pieces(x):
    hi = x.astype(BF)
    return hi, (x - hi.astype(F32)).astype(BF)


def one_hot(rows, first, names):
    at = lax.broadcasted_iota(I32, (rows, names.shape[1]), 0) + first
    return jnp.where(at == names, 1.0, 0.0).astype(BF)


def restraint_kernel(
    send_hbm, coords_hbm, weight_hbm, lists_hbm, counts_hbm, centers_hbm, width_hbm, density_hbm, variance_hbm,
    force_ref, mean_ref,
    coords, weights, centers, width, density, variance, lists, counts, send_rows, send_ref,
    ids, names, ids_smem, pack, received, feats, rates, lines, power, total, model, slots, pulls,
    entries, moments, away, back,
    near_sem, halo_send, halo_recv, rep_send, rep_recv, back_send, back_recv,
):
    rep, me = lax.axis_index("rep"), lax.axis_index("sp")
    rep_peers = [(lax.rem(rep + d, 8), me) for d in range(1, 8)]
    barrier = pltpu.get_barrier_semaphore()
    for peer in [sp_peer(o) for o in OFFSETS] + rep_peers:
        pl.semaphore_signal(barrier, inc=1, device_id=peer, device_id_type=MESH)
    near = [
        pltpu.make_async_copy(src, dst, near_sem.at[i])
        for i, (src, dst) in enumerate((
            (send_hbm, send_ref),
            (coords_hbm, coords),
            (weight_hbm, weights.at[pl.ds(0, OWN)]),
            (lists_hbm, lists),
            (counts_hbm, counts),
            (centers_hbm, centers),
            (width_hbm, width),
            (density_hbm, density),
            (variance_hbm, variance),
            (send_hbm, send_rows),
        ))
    ]
    for copy in near:
        copy.start()
    for copy in near[:3]:
        copy.wait()

    halo_copies = []
    for p, offset in enumerate(OFFSETS):
        to = lax.rem(me + 16 - offset, 16)
        for k in range(CAP):
            b = send_ref[to, k]
            for c in range(3):
                row = (p * 4 + c) * CAP + k
                pack[row : row + 1, :] = coords[c, pl.ds(b, 1), :]
            row = (p * 4 + 3) * CAP + k
            pack[row : row + 1, :] = weights[pl.ds(b, 1), :]
        if p == 0:
            pl.semaphore_wait(barrier, len(OFFSETS) + 7)
        copy = pltpu.make_async_remote_copy(
            src_ref=pack.at[pl.ds(p * 4 * CAP, 4 * CAP)],
            dst_ref=received.at[pl.ds(p * 4 * CAP, 4 * CAP)],
            send_sem=halo_send.at[p],
            recv_sem=halo_recv.at[p],
            device_id=sp_peer(16 - offset),
            device_id_type=MESH,
        )
        copy.start()
        halo_copies.append(copy)

    for copy in near[3:]:
        copy.wait()
    table_ids(lists, counts, ids)
    to_smem = pltpu.make_async_copy(ids, ids_smem, near_sem.at[10])
    to_smem.start()
    put_rates(centers, width, rates, lines)
    for g in range(GROUPS):
        for j in range(TILES_OF):
            names[g : g + 1, LIST * j : LIST * j + LIST] = ids[TILES_OF * g + j : TILES_OF * g + j + 1, :]
    weights[TABLE:ROWS, :] = jnp.zeros((ROWS - TABLE, 128), F32)
    for b in range(TABLE, ROWS):
        feats[b] = jnp.zeros((16, 128), BF)

    def own_features(i, carry):
        for u in range(4):
            b = pl.multiple_of(32 * i + 8 * u, 8)
            put_features([coords[c, pl.ds(b, 8), :] for c in range(3)], feats, b, lines, u)
        return carry

    lax.fori_loop(0, OWN // 32, own_features, 0)
    to_smem.wait()
    for p, copy in enumerate(halo_copies):
        copy.wait()
        for h in range(CAP // 8):
            rows = [
                received[(p * 4 + c) * CAP + 8 * h : (p * 4 + c) * CAP + 8 * h + 8, :]
                for c in range(4)
            ]
            first = OWN + p * CAP + 8 * h
            put_features(rows[:3], feats, first, lines, (2 * p + h) % 4)
            weights[first : first + 8, :] = rows[3]
    lines[0 : TILES_OF * 16, :] = jnp.zeros((TILES_OF * 16, 128), F32)
    ones = jnp.ones((16, 256), BF)

    def replicas(group):
        rows = pl.ds(pl.multiple_of(TILES_OF * group, 8), TILES_OF)
        return [
            pltpu.make_async_remote_copy(
                src_ref=model.at[rows],
                dst_ref=slots.at[rep, rows],
                send_sem=rep_send.at[group, d],
                recv_sem=rep_recv.at[group, d],
                device_id=peer,
                device_id_type=MESH,
            )
            for d, peer in enumerate(rep_peers)
        ]

    def first_pass(group):
        def body(i, carry):
            tile = TILES_OF * group + BUNCH * i
            place = STEPS_OF * lax.rem(group, 2) + BUNCH * (LIST // 2) * i
            for j in range(BUNCH):
                for s in range(LIST // 2):
                    b1, b2 = ids_smem[tile + j, 2 * s], ids_smem[tile + j, 2 * s + 1]
                    pair = jnp.concatenate([feats[b1], feats[b2]], axis=1)
                    k = jnp.exp2(
                        jnp.dot(
                            rates[tile + j],
                            jnp.concatenate([pair, pair, ones], axis=0),
                            preferred_element_type=F32,
                        )
                    )
                    power[place + j * (LIST // 2) + s] = k
                    more = (
                        k[:, :128] * weights[pl.ds(b1, 1), :] + k[:, 128:] * weights[pl.ds(b2, 1), :]
                    )
                    if s == 0:
                        total[j] = more
                    else:
                        total[j] += more
            for j in range(BUNCH):
                model[pl.ds(tile + j, 1), :] = jnp.sum(total[j], axis=-1)[None, :]
            return carry

        lax.fori_loop(0, TILES_OF // BUNCH, body, 0)
        for copy in replicas(group):
            copy.start()

    def second_pass(group):
        rows = pl.ds(pl.multiple_of(TILES_OF * group, 8), TILES_OF)
        slots[rep, rows] = model[rows, :]
        for copy in replicas(group):
            copy.wait()
        sum_ = slots[0, rows]
        for r in range(1, 8):
            sum_ = sum_ + slots[r, rows]
        mean = sum_ * 0.125
        mean_ref[rows, :] = mean
        rate = (mean - density[rows, :]) / variance[rows, :] * width[rows, :]
        for row, value in enumerate([rate] + [rate * centers[c, rows] for c in range(3)]):
            hi = value.astype(BF).astype(F32)
            lines[pl.ds(row, 8, stride=16), :] = hi
            lines[pl.ds(4 + row, 8, stride=16), :] = value - hi
        for j in range(TILES_OF):
            eight = lines[16 * j : 16 * j + 16, :].astype(BF)
            pulls[j] = jnp.concatenate([eight, eight], axis=1)

        def body(i, carry):
            place = STEPS_OF * lax.rem(group, 2) + BUNCH * (LIST // 2) * i
            entry = (TILES_OF * group + BUNCH * i) * LIST
            for j in range(BUNCH):
                for s in range(LIST // 2):
                    k = power[place + j * (LIST // 2) + s]
                    hi, lo = two_pieces(k)
                    both = jnp.dot(
                        pulls[BUNCH * i + j],
                        jnp.concatenate([hi, lo], axis=0),
                        preferred_element_type=F32,
                    )
                    at = entry + j * LIST + 2 * s
                    entries[at] = both[:8, :128]
                    entries[at + 1] = both[:8, 128:]
            return carry

        lax.fori_loop(0, TILES_OF // BUNCH, body, 0)

    def turn(i, carry):
        @pl.when(i < GROUPS)
        def _():
            first_pass(i)

        @pl.when(i > 0)
        def _():
            second_pass(i - 1)

        return carry

    lax.fori_loop(0, GROUPS + 1, turn, 0)

    def collect(rows, first):
        def body(g, carry):
            hot = one_hot(rows, first, names[pl.ds(g, 1), :])
            for half in range(2):
                parts = []
                for c in (2 * half, 2 * half + 1):
                    x = sum_rows(g, c)
                    parts.append(two_pieces(x))
                hi = jnp.concatenate([parts[0][0], parts[1][0]], axis=1)
                lo = jnp.concatenate([parts[0][1], parts[1][1]], axis=1)
                got = jnp.dot(hot, hi, preferred_element_type=F32) + jnp.dot(
                    hot, lo, preferred_element_type=F32
                )
                for q in range(2):
                    moments[2 * half + q, first : first + rows, :] += got[:, 128 * q : 128 * q + 128]
            return carry

        def sum_rows(g, c):
            flat = entries.reshape(TILES * LIST * 8, 128)
            at = pl.multiple_of(g * PAIRS_OF * 8, 8)
            return (
                flat[pl.ds(at + c, PAIRS_OF, stride=8), :]
                + flat[pl.ds(at + 4 + c, PAIRS_OF, stride=8), :]
            )

        for c in range(4):
            moments[c, first : first + rows, :] = jnp.zeros((rows, 128), F32)
        lax.fori_loop(0, GROUPS, body, 0)

    collect(HALO, OWN)
    for p in range(len(OFFSETS)):
        from_ = OWN + p * CAP
        at = p * 4 * CAP
        twice = 2.0 * received[at + 3 * CAP : at + 4 * CAP, :]
        for c in range(3):
            xyz = received[at + c * CAP : at + c * CAP + CAP, :]
            to = p * BACK + c * CAP
            away[to : to + CAP, :] = twice * (
                xyz * moments[0, from_ : from_ + CAP, :] - moments[1 + c, from_ : from_ + CAP, :]
            )
    back_copies = []
    for p, offset in enumerate(OFFSETS):
        copy = pltpu.make_async_remote_copy(
            src_ref=away.at[pl.ds(p * BACK, BACK)],
            dst_ref=back.at[pl.ds(p * BACK, BACK)],
            send_sem=back_send.at[p],
            recv_sem=back_recv.at[p],
            device_id=sp_peer(offset),
            device_id_type=MESH,
        )
        copy.start()
        back_copies.append(copy)
    collect(OWN, 0)
    for copy in back_copies:
        copy.wait()
    sent = [send_rows[pl.ds(lax.rem(me + 16 - offset, 16), 1), :] for offset in OFFSETS]
    hot = one_hot(OWN, 0, jnp.concatenate(sent + [jnp.full((1, 128 - HALO), -1, I32)], axis=1))
    twice = 2.0 * weights[0:OWN, :]
    for c in range(3):
        rows = [back[p * BACK + c * CAP : p * BACK + c * CAP + CAP, :] for p in range(len(OFFSETS))]
        hi, lo = two_pieces(jnp.concatenate(rows + [jnp.zeros((128 - HALO, 128), F32)], axis=0))
        got = jnp.dot(
            jnp.concatenate([hot, hot], axis=1),
            jnp.concatenate([hi, lo], axis=0),
            preferred_element_type=F32,
        )
        force_ref[c] = got + twice * (coords[c] * moments[0, 0:OWN, :] - moments[1 + c, 0:OWN, :])


def restraint(*given):
    dma = pltpu.SemaphoreType.DMA
    peers = len(OFFSETS)
    tiles = pltpu.VMEM((TILES, 128), F32)
    return pl.pallas_call(
        restraint_kernel,
        out_shape=(
            jax.ShapeDtypeStruct((3, OWN, 128), F32),
            jax.ShapeDtypeStruct((TILES, 128), F32),
        ),
        in_specs=[HBM] * 9,
        out_specs=(VMEM,) * 2,
        scratch_shapes=[
            pltpu.VMEM((3, OWN, 128), F32),
            pltpu.VMEM((ROWS, 128), F32),
            pltpu.VMEM((3, TILES, 128), F32),
            tiles,
            tiles,
            tiles,
            pltpu.VMEM((TILES, LIST), I32),
            pltpu.VMEM((1, TILES), I32),
            pltpu.VMEM((16, CAP), I32),
            pltpu.SMEM((16, CAP), I32),
            pltpu.VMEM((TILES, LIST), I32),
            pltpu.VMEM((GROUPS, PAIRS_OF), I32),
            pltpu.SMEM((TILES, LIST), I32),
            pltpu.VMEM((4 * HALO, 128), F32),
            pltpu.VMEM((4 * HALO, 128), F32),
            pltpu.VMEM((ROWS, 16, 128), BF),
            pltpu.VMEM((TILES, 128, DEPTH), BF),
            pltpu.VMEM((TILES * DEPTH, 128), F32),
            pltpu.VMEM((2 * STEPS_OF, 128, 256), F32),
            pltpu.VMEM((BUNCH, 128, 128), F32),
            tiles,
            pltpu.VMEM((8, TILES, 128), F32),
            pltpu.VMEM((TILES_OF, 16, 256), BF),
            pltpu.VMEM((TILES * LIST, 8, 128), F32),
            pltpu.VMEM((4, TABLE, 128), F32),
            pltpu.VMEM((3 * HALO, 128), F32),
            pltpu.VMEM((3 * HALO, 128), F32),
            dma((11,)),
            dma((peers,)),
            dma((peers,)),
            dma((GROUPS, 7)),
            dma((GROUPS, 7)),
            dma((peers,)),
            dma((peers,)),
        ],
        compiler_params=params(58, 0),
        name="restraint",
    )(*given)


def local(
    coords, atom_weight, centers, inv_width, density, variance, tile_blocks, tile_counts, send_blocks
):
    own, send = jnp.transpose(coords[0], (1, 0, 2)), send_blocks[0]
    centers = jnp.transpose(centers, (1, 0, 2))
    given = (send, own, atom_weight, tile_blocks, tile_counts[None], centers, inv_width, density, variance)
    forces, mean = restraint(*[pltpu.with_memory_space_constraint(x, pltpu.HBM) for x in given])
    return jnp.transpose(forces, (1, 0, 2))[None], mean


def solution(mesh):
    return jax.shard_map(
        local,
        mesh=mesh,
        in_specs=(
            P("rep", "sp", None, None),
            P("sp", None),
            P("sp", None, None),
            P("sp", None),
            P("sp", None),
            P("sp", None),
            P("sp", None),
            P("sp"),
            P("sp", None, None),
        ),
        out_specs=(P("rep", "sp", None, None), P("sp", None)),
        check_vma=False,
    )
```

time: 690 us -> 47.7 us (0.07); the launches traced: 678 us -> 47.5 us
  matrix products: 231 us -> 0 us
  waiting for transfers between devices: 205 us -> 0 us
  other arithmetic: 80.3 us -> 0 us
  local copies, waits for them, and re-layouts: 74.4 us -> 2.68 us
  blocking collectives: 50.7 us -> 0 us
  Pallas kernels: 0 us -> 44.2 us
  loops' own time: 22 us -> 0 us
  between operations: 14 us -> 0.65 us
    dot_general x12 -> x0, matrix products: 231 us -> none  [the longest x4 111 us: model_intersection(): jnp.einsum('gja,ja->g', kernel, block_weight, precision=lax.Precision.HIG...]
    all_gather x2 -> x0, waiting for transfers between devices: 113 us -> none  [the longest x1 89.5 us: local(): lax.all_gather(own_coords, 'sp', axis=0, tiled=True)]
    reduce_scatter x1 -> x0, waiting for transfers between devices: 91.9 us -> none  [local(): lax.psum_scatter(whole_forces, 'sp', scatter_dimension=0, tiled=True)]
    pallas_call x0 -> x1, Pallas kernels: none -> 44.2 us  [restraint(): pl.pallas_call(restraint_kernel, out_shape=(jax.ShapeDtypeStruct((3, OWN,...]
    exp x4 -> x0, other arithmetic: 39.8 us -> none  [gaussian_kernel(): return jnp.exp(-width_rate[:, None, None] * dist_sq)]
    all_gather x2 -> x0, local copies, waits for them, and re-layouts: 28 us -> none  [local(): lax.all_gather(own_coords, 'sp', axis=0, tiled=True)]
    psum x1 -> x0, blocking collectives: 25.6 us -> none  [local(): mean_model = lax.psum(model, 'rep') / rep_count]
    scatter-add x5 -> x0, other arithmetic: 25.6 us -> none  [the longest x4 17.7 us: second_pass(): return (carry.at[lists_here.reshape(-1)].add(pulls.reshape(-1, 384)), None)]
  transfers between devices with their start and end apart: 3 -> 0, of which waited for: 3 -> 0; matrix products, arithmetic and copies ran while one was open for 2% -> 0% of each run, Pallas kernels for 0% -> 0%
where the time goes in v4:
time: 47.7 us; the launch traced here: 47.5 us
  Pallas kernels  44.2 us (93%)
  local copies, waits for them, and re-layouts  2.68 us (6%)
  between operations  0.65 us (1%)
    pallas_call x1, Pallas kernels, restraint(): pl.pallas_call(restraint_kernel, out_shape=(jax.ShapeDtypeStruct((3, OWN,...  44.2 us
    unnamed x4, local copies, waits for them, and re-layouts  2.68 us

profile of v4, /device:TPU:0, one launch (start us, length us, event | category | flops | bytes accessed | tf_op | source)
XLA Modules:
  0.0 47.5 jit_solution(3984582999861012239)
XLA Ops:
  0.6 44.2 %restraint.1 = (f32[3,512,128]{2,1,0:T(8,128)}, f32[32,128]{1,0:T(8,128)}) custom-call(s32[16,16]{1,0:T(8,128)} %bitcast.12, f32[3,512,128]{2,1,0:T(8,128)} %bitcast.10, f32[512,128]{1,0:T(8,128)} %weight_hbm.1, s32[32,32]{1,0:T(8,128)} %lists_hbm.1, s32[1,32]{1,0:T(1,128)} %bitcast.13, f32[3,32,128]{2,1,0:T(8,128)} %bitcast.11, f32[32,128]{1,0:T(8,128)} %width_hbm.1, ...), custom_call_target="tpu_custom_call" | custom-call | tf_op jit(solution)/shard_map/restraint/pallas_call | solution.py:371
  44.8 0.0 copy-start
  44.9 2.1 %copy.13 = f32[1,512,3,128]{3,1,2,0:T(8,128)} copy(f32[1,512,3,128]{3,1,2,0:T(8,128)} %bitcast.9) | data formatting | bytes 1572864
  46.9 0.0 copy-done
  46.9 0.6 %copy.14 = f32[32,128]{1,0:T(8,128)} copy(f32[32,128]{1,0:T(8,128)S(1)} %copy-done) | data formatting | bytes 32768
Async XLA Ops:
  44.8 2.1 %copy-start = (f32[32,128]{1,0:T(8,128)S(1)}, f32[32,128]{1,0:T(8,128)}, u32[]{:S(2)}) copy-start(f32[32,128]{1,0:T(8,128)} %get-tuple-element.9) | copy-start | bytes 49156

commit v5 on v4

--- a/solution.py
+++ b/solution.py
@@ -25,11 +25,12 @@
 TILES = 32
 LIST = 32
 STEPS = TILES * LIST // 2
-GROUPS = 4
+GROUPS = 8
+LAG = 4
 TILES_OF = TILES // GROUPS
 STEPS_OF = STEPS // GROUPS
-PAIRS_OF = TILES_OF * LIST
-BUNCH = 4
+PAIRS_OF = 256
+BATCHES = TILES * LIST // PAIRS_OF
 BACK = 3 * CAP
 DEPTH = 48
 LOG2E = 1.4426950408889634
@@ -113,7 +114,7 @@
     send_hbm, coords_hbm, weight_hbm, lists_hbm, counts_hbm, centers_hbm, width_hbm, density_hbm, variance_hbm,
     force_ref, mean_ref,
     coords, weights, centers, width, density, variance, lists, counts, send_rows, send_ref,
-    ids, names, ids_smem, pack, received, feats, rates, lines, power, total, model, slots, pulls,
+    ids, names, ids_smem, pack, received, feats, rates, lines, power, total, model, slots, means,
     entries, moments, away, back,
     near_sem, halo_send, halo_recv, rep_send, rep_recv, back_send, back_recv,
 ):
@@ -171,9 +172,9 @@
     to_smem = pltpu.make_async_copy(ids, ids_smem, near_sem.at[10])
     to_smem.start()
     put_rates(centers, width, rates, lines)
-    for g in range(GROUPS):
-        for j in range(TILES_OF):
-            names[g : g + 1, LIST * j : LIST * j + LIST] = ids[TILES_OF * g + j : TILES_OF * g + j + 1, :]
+    for t in range(TILES):
+        g, j = divmod(t, PAIRS_OF // LIST)
+        names[g : g + 1, LIST * j : LIST * j + LIST] = ids[t : t + 1, :]
     weights[TABLE:ROWS, :] = jnp.zeros((ROWS - TABLE, 128), F32)
     for b in range(TABLE, ROWS):
         feats[b] = jnp.zeros((16, 128), BF)
@@ -200,11 +201,10 @@
     ones = jnp.ones((16, 256), BF)
 
     def replicas(group):
-        rows = pl.ds(pl.multiple_of(TILES_OF * group, 8), TILES_OF)
         return [
             pltpu.make_async_remote_copy(
-                src_ref=model.at[rows],
-                dst_ref=slots.at[rep, rows],
+                src_ref=model.at[group],
+                dst_ref=slots.at[rep, group],
                 send_sem=rep_send.at[group, d],
                 recv_sem=rep_recv.at[group, d],
                 device_id=peer,
@@ -214,86 +214,74 @@
         ]
 
     def first_pass(group):
-        def body(i, carry):
-            tile = TILES_OF * group + BUNCH * i
-            place = STEPS_OF * lax.rem(group, 2) + BUNCH * (LIST // 2) * i
-            for j in range(BUNCH):
-                for s in range(LIST // 2):
-                    b1, b2 = ids_smem[tile + j, 2 * s], ids_smem[tile + j, 2 * s + 1]
-                    pair = jnp.concatenate([feats[b1], feats[b2]], axis=1)
-                    k = jnp.exp2(
-                        jnp.dot(
-                            rates[tile + j],
-                            jnp.concatenate([pair, pair, ones], axis=0),
-                            preferred_element_type=F32,
-                        )
+        tile = TILES_OF * group
+        place = STEPS_OF * lax.rem(group, LAG + 1)
+        for j in range(TILES_OF):
+            for s in range(LIST // 2):
+                b1, b2 = ids_smem[tile + j, 2 * s], ids_smem[tile + j, 2 * s + 1]
+                pair = jnp.concatenate([feats[b1], feats[b2]], axis=1)
+                k = jnp.exp2(
+                    jnp.dot(
+                        rates[tile + j],
+                        jnp.concatenate([pair, pair, ones], axis=0),
+                        preferred_element_type=F32,
                     )
-                    power[place + j * (LIST // 2) + s] = k
-                    more = (
-                        k[:, :128] * weights[pl.ds(b1, 1), :] + k[:, 128:] * weights[pl.ds(b2, 1), :]
-                    )
-                    if s == 0:
-                        total[j] = more
-                    else:
-                        total[j] += more
-            for j in range(BUNCH):
-                model[pl.ds(tile + j, 1), :] = jnp.sum(total[j], axis=-1)[None, :]
-            return carry
-
-        lax.fori_loop(0, TILES_OF // BUNCH, body, 0)
+                )
+                power[place + j * (LIST // 2) + s] = k
+                more = (
+                    k[:, :128] * weights[pl.ds(b1, 1), :] + k[:, 128:] * weights[pl.ds(b2, 1), :]
+                )
+                if s == 0:
+                    total[j] = more
+                else:
+                    total[j] += more
+        for j in range(TILES_OF):
+            model[group, j : j + 1, :] = jnp.sum(total[j], axis=-1)[None, :]
         for copy in replicas(group):
             copy.start()
 
     def second_pass(group):
-        rows = pl.ds(pl.multiple_of(TILES_OF * group, 8), TILES_OF)
-        slots[rep, rows] = model[rows, :]
+        rows = pl.ds(pl.multiple_of(TILES_OF * group, TILES_OF), TILES_OF)
+        slots[rep, group] = model[group]
         for copy in replicas(group):
             copy.wait()
-        sum_ = slots[0, rows]
+        sum_ = slots[0, group]
         for r in range(1, 8):
-            sum_ = sum_ + slots[r, rows]
+            sum_ = sum_ + slots[r, group]
         mean = sum_ * 0.125
-        mean_ref[rows, :] = mean
+        means[group] = mean
         rate = (mean - density[rows, :]) / variance[rows, :] * width[rows, :]
         for row, value in enumerate([rate] + [rate * centers[c, rows] for c in range(3)]):
             hi = value.astype(BF).astype(F32)
-            lines[pl.ds(row, 8, stride=16), :] = hi
-            lines[pl.ds(4 + row, 8, stride=16), :] = value - hi
+            lines[pl.ds(row, TILES_OF, stride=16), :] = hi
+            lines[pl.ds(4 + row, TILES_OF, stride=16), :] = value - hi
+        place = STEPS_OF * lax.rem(group, LAG + 1)
+        entry = TILES_OF * group * LIST
         for j in range(TILES_OF):
             eight = lines[16 * j : 16 * j + 16, :].astype(BF)
-            pulls[j] = jnp.concatenate([eight, eight], axis=1)
-
-        def body(i, carry):
-            place = STEPS_OF * lax.rem(group, 2) + BUNCH * (LIST // 2) * i
-            entry = (TILES_OF * group + BUNCH * i) * LIST
-            for j in range(BUNCH):
-                for s in range(LIST // 2):
-                    k = power[place + j * (LIST // 2) + s]
-                    hi, lo = two_pieces(k)
-                    both = jnp.dot(
-                        pulls[BUNCH * i + j],
-                        jnp.concatenate([hi, lo], axis=0),
-                        preferred_element_type=F32,
-                    )
-                    at = entry + j * LIST + 2 * s
-                    entries[at] = both[:8, :128]
-                    entries[at + 1] = both[:8, 128:]
-            return carry
-
-        lax.fori_loop(0, TILES_OF // BUNCH, body, 0)
+            pull = jnp.concatenate([eight, eight], axis=1)
+            for s in range(LIST // 2):
+                hi, lo = two_pieces(power[place + j * (LIST // 2) + s])
+                both = jnp.dot(pull, jnp.concatenate([hi, lo], axis=0), preferred_element_type=F32)
+                four = both[:4] + both[4:8]
+                at = entry + j * LIST + 2 * s
+                entries[at] = four[:, :128]
+                entries[at + 1] = four[:, 128:]
 
     def turn(i, carry):
         @pl.when(i < GROUPS)
         def _():
             first_pass(i)
 
-        @pl.when(i > 0)
+        @pl.when(i >= LAG)
         def _():
-            second_pass(i - 1)
+            second_pass(i - LAG)
 
         return carry
 
-    lax.fori_loop(0, GROUPS + 1, turn, 0)
+    lax.fori_loop(0, GROUPS + LAG, turn, 0)
+    for g in range(GROUPS):
+        mean_ref[TILES_OF * g : TILES_OF * g + TILES_OF, :] = means[g]
 
     def collect(rows, first):
         def body(g, carry):
@@ -313,16 +301,12 @@
             return carry
 
         def sum_rows(g, c):
-            flat = entries.reshape(TILES * LIST * 8, 128)
-            at = pl.multiple_of(g * PAIRS_OF * 8, 8)
-            return (
-                flat[pl.ds(at + c, PAIRS_OF, stride=8), :]
-                + flat[pl.ds(at + 4 + c, PAIRS_OF, stride=8), :]
-            )
+            flat = entries.reshape(TILES * LIST * 4, 128)
+            return flat[pl.ds(pl.multiple_of(g * PAIRS_OF * 4, 8) + c, PAIRS_OF, stride=4), :]
 
         for c in range(4):
             moments[c, first : first + rows, :] = jnp.zeros((rows, 128), F32)
-        lax.fori_loop(0, GROUPS, body, 0)
+        lax.fori_loop(0, BATCHES, body, 0)
 
     collect(HALO, OWN)
     for p in range(len(OFFSETS)):
@@ -388,19 +372,19 @@
             pltpu.VMEM((16, CAP), I32),
             pltpu.SMEM((16, CAP), I32),
             pltpu.VMEM((TILES, LIST), I32),
-            pltpu.VMEM((GROUPS, PAIRS_OF), I32),
+            pltpu.VMEM((BATCHES, PAIRS_OF), I32),
             pltpu.SMEM((TILES, LIST), I32),
             pltpu.VMEM((4 * HALO, 128), F32),
             pltpu.VMEM((4 * HALO, 128), F32),
             pltpu.VMEM((ROWS, 16, 128), BF),
             pltpu.VMEM((TILES, 128, DEPTH), BF),
             pltpu.VMEM((TILES * DEPTH, 128), F32),
-            pltpu.VMEM((2 * STEPS_OF, 128, 256), F32),
-            pltpu.VMEM((BUNCH, 128, 128), F32),
-            tiles,
-            pltpu.VMEM((8, TILES, 128), F32),
-            pltpu.VMEM((TILES_OF, 16, 256), BF),
-            pltpu.VMEM((TILES * LIST, 8, 128), F32),
+            pltpu.VMEM(((LAG + 1) * STEPS_OF, 128, 256), F32),
+            pltpu.VMEM((TILES_OF, 128, 128), F32),
+            pltpu.VMEM((GROUPS, TILES_OF, 128), F32),
+            pltpu.VMEM((8, GROUPS, TILES_OF, 128), F32),
+            pltpu.VMEM((GROUPS, TILES_OF, 128), F32),
+            pltpu.VMEM((TILES * LIST, 4, 128), F32),
             pltpu.VMEM((4, TABLE, 128), F32),
             pltpu.VMEM((3 * HALO, 128), F32),
             pltpu.VMEM((3 * HALO, 128), F32),
@@ -412,9 +396,40 @@
             dma((peers,)),
             dma((peers,)),
         ],
-        compiler_params=params(58, 0),
+        compiler_params=params(52, 0),
         name="restraint",
     )(*given)
+
+
+def store_kernel(force_ref, mean_ref, force_hbm, mean_hbm, sems):
+    copies = [pltpu.make_async_copy(mean_ref, mean_hbm, sems.at[0])]
+    for c in range(3):
+        for h in range(2):
+            rows = pl.ds(OWN // 2 * h, OWN // 2)
+            copies.append(
+                pltpu.make_async_copy(
+                    force_ref.at[c, rows], force_hbm.at[c, rows], sems.at[1 + 2 * c + h]
+                )
+            )
+    for copy in copies:
+        copy.start()
+    for copy in copies:
+        copy.wait()
+
+
+def store(forces, mean):
+    return pl.pallas_call(
+        store_kernel,
+        out_shape=(
+            jax.ShapeDtypeStruct((3, OWN, 128), F32),
+            jax.ShapeDtypeStruct((TILES, 128), F32),
+        ),
+        in_specs=[VMEM] * 2,
+        out_specs=(HBM,) * 2,
+        scratch_shapes=[pltpu.SemaphoreType.DMA((7,))],
+        compiler_params=params(2),
+        name="store",
+    )(forces, mean)
 
 
 def local(
@@ -423,7 +438,9 @@
     own, send = jnp.transpose(coords[0], (1, 0, 2)), send_blocks[0]
     centers = jnp.transpose(centers, (1, 0, 2))
     given = (send, own, atom_weight, tile_blocks, tile_counts[None], centers, inv_width, density, variance)
-    forces, mean = restraint(*[pltpu.with_memory_space_constraint(x, pltpu.HBM) for x in given])
+    forces, mean = store(
+        *restraint(*[pltpu.with_memory_space_constraint(x, pltpu.HBM) for x in given])
+    )
     return jnp.transpose(forces, (1, 0, 2))[None], mean
 
 

time: 47.7 us -> 42.9 us (0.90)
  local copies, waits for them, and re-layouts: 2.68 us -> 0 us
  Pallas kernels: 44.2 us -> 42.1 us
    pallas_call x1, Pallas kernels: 44.2 us -> 41.2 us  [restraint(): pl.pallas_call(restraint_kernel, out_shape=(jax.ShapeDtypeStruct((3, OWN,...]
    unnamed x4 -> x0, local copies, waits for them, and re-layouts: 2.68 us -> none
    pallas_call x0 -> x1, Pallas kernels: none -> 0.94 us  [store(): pl.pallas_call(store_kernel, out_shape=(jax.ShapeDtypeStruct((3, OWN, 128...]
where the time goes in v5:
time: 42.9 us; the launch traced here: 42.7 us
  Pallas kernels  42.1 us (98%)
  between operations  0.64 us (1%)
    pallas_call x1, Pallas kernels, restraint(): pl.pallas_call(restraint_kernel, out_shape=(jax.ShapeDtypeStruct((3, OWN,...  41.2 us
    pallas_call x1, Pallas kernels, store(): pl.pallas_call(store_kernel, out_shape=(jax.ShapeDtypeStruct((3, OWN, 128...  0.94 us

profile of v5, /device:TPU:0, one launch (start us, length us, event | category | flops | bytes accessed | tf_op | source)
XLA Modules:
  0.0 42.7 jit_solution(3835139542338630557)
XLA Ops:
  0.6 41.2 %restraint.1 = (f32[3,512,128]{2,1,0:T(8,128)S(1)}, f32[32,128]{1,0:T(8,128)S(1)}) custom-call(s32[16,16]{1,0:T(8,128)} %bitcast.11, f32[3,512,128]{2,1,0:T(8,128)} %bitcast.9, f32[512,128]{1,0:T(8,128)} %weight_hbm.1, s32[32,32]{1,0:T(8,128)} %lists_hbm.1, s32[1,32]{1,0:T(1,128)} %bitcast.12, f32[3,32,128]{2,1,0:T(8,128)} %bitcast.10, f32[32,128]{1,0:T(8,128)} %width_hbm.1, ...), custom_call_target="tpu_custom_call" | custom-call | tf_op jit(solution)/shard_map/restraint/pallas_call | solution.py:355
  41.8 0.9 %store.1 = (f32[3,512,128]{2,1,0:T(8,128)}, f32[32,128]{1,0:T(8,128)}) custom-call(f32[3,512,128]{2,1,0:T(8,128)S(1)} %get-tuple-element.6.force_ref, f32[32,128]{1,0:T(8,128)S(1)} %get-tuple-element.7.mean_ref), custom_call_target="tpu_custom_call" | custom-call | tf_op jit(solution)/shard_map/store/pallas_call | solution.py:421

commit v6 on v5

--- a/solution.py
+++ b/solution.py
@@ -17,6 +17,9 @@
 
 OFFSETS = (1, 2, 3, 8, 13, 14, 15)
 CAP = 16
+SENT_ORDER = (0, 1, 2, 3, 4, 5, 6)
+WAIT_ORDER = (0, 6, 3, 2, 4, 1, 5)
+BACK_ORDER = (1, 0, 2, 3, 5, 4, 6)
 OWN = 512
 HALO = len(OFFSETS) * CAP
 TABLE = OWN + HALO
@@ -115,7 +118,7 @@
     force_ref, mean_ref,
     coords, weights, centers, width, density, variance, lists, counts, send_rows, send_ref,
     ids, names, ids_smem, pack, received, feats, rates, lines, power, total, model, slots, means,
-    entries, moments, away, back,
+    entries, moments, away, back, hots,
     near_sem, halo_send, halo_recv, rep_send, rep_recv, back_send, back_recv,
 ):
     rep, me = lax.axis_index("rep"), lax.axis_index("sp")
@@ -127,7 +130,9 @@
         pltpu.make_async_copy(src, dst, near_sem.at[i])
         for i, (src, dst) in enumerate((
             (send_hbm, send_ref),
-            (coords_hbm, coords),
+            (coords_hbm.at[0], coords.at[0]),
+            (coords_hbm.at[1], coords.at[1]),
+            (coords_hbm.at[2], coords.at[2]),
             (weight_hbm, weights.at[pl.ds(0, OWN)]),
             (lists_hbm, lists),
             (counts_hbm, counts),
@@ -140,11 +145,12 @@
     ]
     for copy in near:
         copy.start()
-    for copy in near[:3]:
+    for copy in near[:5]:
         copy.wait()
 
-    halo_copies = []
-    for p, offset in enumerate(OFFSETS):
+    halo_copies = {}
+    for p in SENT_ORDER:
+        offset = OFFSETS[p]
         to = lax.rem(me + 16 - offset, 16)
         for k in range(CAP):
             b = send_ref[to, k]
@@ -153,8 +159,9 @@
                 pack[row : row + 1, :] = coords[c, pl.ds(b, 1), :]
             row = (p * 4 + 3) * CAP + k
             pack[row : row + 1, :] = weights[pl.ds(b, 1), :]
-        if p == 0:
-            pl.semaphore_wait(barrier, len(OFFSETS) + 7)
+    pl.semaphore_wait(barrier, len(OFFSETS) + 7)
+    for p in SENT_ORDER:
+        offset = OFFSETS[p]
         copy = pltpu.make_async_remote_copy(
             src_ref=pack.at[pl.ds(p * 4 * CAP, 4 * CAP)],
             dst_ref=received.at[pl.ds(p * 4 * CAP, 4 * CAP)],
@@ -164,12 +171,12 @@
             device_id_type=MESH,
         )
         copy.start()
-        halo_copies.append(copy)
-
-    for copy in near[3:]:
+        halo_copies[p] = copy
+
+    for copy in near[5:]:
         copy.wait()
     table_ids(lists, counts, ids)
-    to_smem = pltpu.make_async_copy(ids, ids_smem, near_sem.at[10])
+    to_smem = pltpu.make_async_copy(ids, ids_smem, near_sem.at[12])
     to_smem.start()
     put_rates(centers, width, rates, lines)
     for t in range(TILES):
@@ -187,8 +194,8 @@
 
     lax.fori_loop(0, OWN // 32, own_features, 0)
     to_smem.wait()
-    for p, copy in enumerate(halo_copies):
-        copy.wait()
+    for p in WAIT_ORDER:
+        halo_copies[p].wait()
         for h in range(CAP // 8):
             rows = [
                 received[(p * 4 + c) * CAP + 8 * h : (p * 4 + c) * CAP + 8 * h + 8, :]
@@ -320,7 +327,8 @@
                 xyz * moments[0, from_ : from_ + CAP, :] - moments[1 + c, from_ : from_ + CAP, :]
             )
     back_copies = []
-    for p, offset in enumerate(OFFSETS):
+    for p in BACK_ORDER:
+        offset = OFFSETS[p]
         copy = pltpu.make_async_remote_copy(
             src_ref=away.at[pl.ds(p * BACK, BACK)],
             dst_ref=back.at[pl.ds(p * BACK, BACK)],
@@ -332,20 +340,21 @@
         copy.start()
         back_copies.append(copy)
     collect(OWN, 0)
+    twice = 2.0 * weights[0:OWN, :]
+    for c in range(3):
+        force_ref[c] = twice * (coords[c] * moments[0, 0:OWN, :] - moments[1 + c, 0:OWN, :])
+    sent = [send_rows[pl.ds(lax.rem(me + 16 - offset, 16), 1), :] for offset in OFFSETS]
+    hot = one_hot(OWN, 0, jnp.concatenate(sent + [jnp.full((1, 128 - HALO), -1, I32)], axis=1))
+    hots[:, :128] = hot
+    hots[:, 128:] = hot
     for copy in back_copies:
         copy.wait()
-    sent = [send_rows[pl.ds(lax.rem(me + 16 - offset, 16), 1), :] for offset in OFFSETS]
-    hot = one_hot(OWN, 0, jnp.concatenate(sent + [jnp.full((1, 128 - HALO), -1, I32)], axis=1))
-    twice = 2.0 * weights[0:OWN, :]
     for c in range(3):
         rows = [back[p * BACK + c * CAP : p * BACK + c * CAP + CAP, :] for p in range(len(OFFSETS))]
         hi, lo = two_pieces(jnp.concatenate(rows + [jnp.zeros((128 - HALO, 128), F32)], axis=0))
-        got = jnp.dot(
-            jnp.concatenate([hot, hot], axis=1),
-            jnp.concatenate([hi, lo], axis=0),
-            preferred_element_type=F32,
+        force_ref[c] += jnp.dot(
+            hots[...], jnp.concatenate([hi, lo], axis=0), preferred_element_type=F32
         )
-        force_ref[c] = got + twice * (coords[c] * moments[0, 0:OWN, :] - moments[1 + c, 0:OWN, :])
 
 
 def restraint(*given):
@@ -388,7 +397,8 @@
             pltpu.VMEM((4, TABLE, 128), F32),
             pltpu.VMEM((3 * HALO, 128), F32),
             pltpu.VMEM((3 * HALO, 128), F32),
-            dma((11,)),
+            pltpu.VMEM((OWN, 256), BF),
+            dma((13,)),
             dma((peers,)),
             dma((peers,)),
             dma((GROUPS, 7)),
@@ -396,7 +406,7 @@
             dma((peers,)),
             dma((peers,)),
         ],
-        compiler_params=params(52, 0),
+        compiler_params=params(53, 0),
         name="restraint",
     )(*given)
 

time: 42.9 us -> 42.6 us (level)
  no operation moved by 1% of the time
where the time goes in v6:
time: 42.6 us; the launch traced here: 42.4 us
  Pallas kernels  41.8 us (98%)
  between operations  0.64 us (2%)
    pallas_call x1, Pallas kernels, restraint(): pl.pallas_call(restraint_kernel, out_shape=(jax.ShapeDtypeStruct((3, OWN,...  40.9 us
    pallas_call x1, Pallas kernels, store(): pl.pallas_call(store_kernel, out_shape=(jax.ShapeDtypeStruct((3, OWN, 128...  0.94 us

profile of v6, /device:TPU:0, one launch (start us, length us, event | category | flops | bytes accessed | tf_op | source)
XLA Modules:
  0.0 42.4 jit_solution(11297694326038370468)
XLA Ops:
  0.6 40.9 %restraint.1 = (f32[3,512,128]{2,1,0:T(8,128)S(1)}, f32[32,128]{1,0:T(8,128)S(1)}) custom-call(s32[16,16]{1,0:T(8,128)} %bitcast.11, f32[3,512,128]{2,1,0:T(8,128)} %bitcast.9, f32[512,128]{1,0:T(8,128)} %weight_hbm.1, s32[32,32]{1,0:T(8,128)} %lists_hbm.1, s32[1,32]{1,0:T(1,128)} %bitcast.12, f32[3,32,128]{2,1,0:T(8,128)} %bitcast.10, f32[32,128]{1,0:T(8,128)} %width_hbm.1, ...), custom_call_target="tpu_custom_call" | custom-call | tf_op jit(solution)/shard_map/restraint/pallas_call | solution.py:364
  41.5 0.9 %store.1 = (f32[3,512,128]{2,1,0:T(8,128)}, f32[32,128]{1,0:T(8,128)}) custom-call(f32[3,512,128]{2,1,0:T(8,128)S(1)} %get-tuple-element.6.force_ref, f32[32,128]{1,0:T(8,128)S(1)} %get-tuple-element.7.mean_ref), custom_call_target="tpu_custom_call" | custom-call | tf_op jit(solution)/shard_map/store/pallas_call | solution.py:431

commit v7 on v6

--- a/solution.py
+++ b/solution.py
@@ -29,7 +29,7 @@
 LIST = 32
 STEPS = TILES * LIST // 2
 GROUPS = 8
-LAG = 4
+LAG = 5
 TILES_OF = TILES // GROUPS
 STEPS_OF = STEPS // GROUPS
 PAIRS_OF = 256
@@ -220,34 +220,29 @@
             for d, peer in enumerate(rep_peers)
         ]
 
-    def first_pass(group):
-        tile = TILES_OF * group
-        place = STEPS_OF * lax.rem(group, LAG + 1)
-        for j in range(TILES_OF):
-            for s in range(LIST // 2):
-                b1, b2 = ids_smem[tile + j, 2 * s], ids_smem[tile + j, 2 * s + 1]
-                pair = jnp.concatenate([feats[b1], feats[b2]], axis=1)
-                k = jnp.exp2(
-                    jnp.dot(
-                        rates[tile + j],
-                        jnp.concatenate([pair, pair, ones], axis=0),
-                        preferred_element_type=F32,
-                    )
-                )
-                power[place + j * (LIST // 2) + s] = k
-                more = (
-                    k[:, :128] * weights[pl.ds(b1, 1), :] + k[:, 128:] * weights[pl.ds(b2, 1), :]
-                )
-                if s == 0:
-                    total[j] = more
-                else:
-                    total[j] += more
+    def place_of(group):
+        return STEPS_OF * lax.rem(group, LAG)
+
+    def first_step(group, place, j, s):
+        tile = TILES_OF * group + j
+        b1, b2 = ids_smem[tile, 2 * s], ids_smem[tile, 2 * s + 1]
+        pair = jnp.concatenate([feats[b1], feats[b2]], axis=1)
+        rows = jnp.concatenate([pair, pair, ones], axis=0)
+        k = jnp.exp2(jnp.dot(rates[tile], rows, preferred_element_type=F32))
+        power[place + j * (LIST // 2) + s] = k
+        more = k[:, :128] * weights[pl.ds(b1, 1), :] + k[:, 128:] * weights[pl.ds(b2, 1), :]
+        if s == 0:
+            total[j] = more
+        else:
+            total[j] += more
+
+    def send_model(group):
         for j in range(TILES_OF):
             model[group, j : j + 1, :] = jnp.sum(total[j], axis=-1)[None, :]
         for copy in replicas(group):
             copy.start()
 
-    def second_pass(group):
+    def pulls_of(group):
         rows = pl.ds(pl.multiple_of(TILES_OF * group, TILES_OF), TILES_OF)
         slots[rep, group] = model[group]
         for copy in replicas(group):
@@ -262,31 +257,45 @@
             hi = value.astype(BF).astype(F32)
             lines[pl.ds(row, TILES_OF, stride=16), :] = hi
             lines[pl.ds(4 + row, TILES_OF, stride=16), :] = value - hi
-        place = STEPS_OF * lax.rem(group, LAG + 1)
-        entry = TILES_OF * group * LIST
-        for j in range(TILES_OF):
-            eight = lines[16 * j : 16 * j + 16, :].astype(BF)
-            pull = jnp.concatenate([eight, eight], axis=1)
-            for s in range(LIST // 2):
-                hi, lo = two_pieces(power[place + j * (LIST // 2) + s])
-                both = jnp.dot(pull, jnp.concatenate([hi, lo], axis=0), preferred_element_type=F32)
-                four = both[:4] + both[4:8]
-                at = entry + j * LIST + 2 * s
-                entries[at] = four[:, :128]
-                entries[at + 1] = four[:, 128:]
-
-    def turn(i, carry):
-        @pl.when(i < GROUPS)
-        def _():
-            first_pass(i)
-
-        @pl.when(i >= LAG)
-        def _():
-            second_pass(i - LAG)
-
+        eights = [lines[16 * j : 16 * j + 16, :].astype(BF) for j in range(TILES_OF)]
+        return [jnp.concatenate([eight, eight], axis=1) for eight in eights]
+
+    def second_step(group, place, pulls, j, s):
+        hi, lo = two_pieces(power[place + j * (LIST // 2) + s])
+        both = jnp.dot(pulls[j], jnp.concatenate([hi, lo], axis=0), preferred_element_type=F32)
+        four = both[:4] + both[4:8]
+        at = (TILES_OF * group + j) * LIST + 2 * s
+        entries[at] = four[:, :128]
+        entries[at + 1] = four[:, 128:]
+
+    steps = [(j, s) for j in range(TILES_OF) for s in range(LIST // 2)]
+
+    def early(i, carry):
+        place = place_of(i)
+        for j, s in steps:
+            first_step(i, place, j, s)
+        send_model(i)
         return carry
 
-    lax.fori_loop(0, GROUPS + LAG, turn, 0)
+    def middle(i, carry):
+        pulls = pulls_of(i - LAG)
+        place = place_of(i)
+        for j, s in steps:
+            second_step(i - LAG, place, pulls, j, s)
+            first_step(i, place, j, s)
+        send_model(i)
+        return carry
+
+    def late(i, carry):
+        pulls = pulls_of(i - LAG)
+        place = place_of(i)
+        for j, s in steps:
+            second_step(i - LAG, place, pulls, j, s)
+        return carry
+
+    lax.fori_loop(0, LAG, early, 0)
+    lax.fori_loop(LAG, GROUPS, middle, 0)
+    lax.fori_loop(GROUPS, GROUPS + LAG, late, 0)
     for g in range(GROUPS):
         mean_ref[TILES_OF * g : TILES_OF * g + TILES_OF, :] = means[g]
 
@@ -388,7 +397,7 @@
             pltpu.VMEM((ROWS, 16, 128), BF),
             pltpu.VMEM((TILES, 128, DEPTH), BF),
             pltpu.VMEM((TILES * DEPTH, 128), F32),
-            pltpu.VMEM(((LAG + 1) * STEPS_OF, 128, 256), F32),
+            pltpu.VMEM((LAG * STEPS_OF, 128, 256), F32),
             pltpu.VMEM((TILES_OF, 128, 128), F32),
             pltpu.VMEM((GROUPS, TILES_OF, 128), F32),
             pltpu.VMEM((8, GROUPS, TILES_OF, 128), F32),

time: 42.6 us -> 42.1 us (0.988)
  Pallas kernels: 41.8 us -> 41.3 us
    pallas_call x1, Pallas kernels: 40.9 us -> 40.3 us  [restraint(): pl.pallas_call(restraint_kernel, out_shape=(jax.ShapeDtypeStruct((3, OWN,...]
where the time goes in v7:
time: 42.1 us; the launch traced here: 41.9 us
  Pallas kernels  41.3 us (98%)
  between operations  0.64 us (2%)
    pallas_call x1, Pallas kernels, restraint(): pl.pallas_call(restraint_kernel, out_shape=(jax.ShapeDtypeStruct((3, OWN,...  40.3 us
    pallas_call x1, Pallas kernels, store(): pl.pallas_call(store_kernel, out_shape=(jax.ShapeDtypeStruct((3, OWN, 128...  0.94 us

profile of v7, /device:TPU:0, one launch (start us, length us, event | category | flops | bytes accessed | tf_op | source)
XLA Modules:
  0.0 41.9 jit_solution(14843088149602359456)
XLA Ops:
  0.6 40.3 %restraint.1 = (f32[3,512,128]{2,1,0:T(8,128)S(1)}, f32[32,128]{1,0:T(8,128)S(1)}) custom-call(s32[16,16]{1,0:T(8,128)} %bitcast.11, f32[3,512,128]{2,1,0:T(8,128)} %bitcast.9, f32[512,128]{1,0:T(8,128)} %weight_hbm.1, s32[32,32]{1,0:T(8,128)} %lists_hbm.1, s32[1,32]{1,0:T(1,128)} %bitcast.12, f32[3,32,128]{2,1,0:T(8,128)} %bitcast.10, f32[32,128]{1,0:T(8,128)} %width_hbm.1, ...), custom_call_target="tpu_custom_call" | custom-call | tf_op jit(solution)/shard_map/restraint/pallas_call | solution.py:373
  41.0 0.9 %store.1 = (f32[3,512,128]{2,1,0:T(8,128)}, f32[32,128]{1,0:T(8,128)}) custom-call(f32[3,512,128]{2,1,0:T(8,128)S(1)} %get-tuple-element.6.force_ref, f32[32,128]{1,0:T(8,128)S(1)} %get-tuple-element.7.mean_ref), custom_call_target="tpu_custom_call" | custom-call | tf_op jit(solution)/shard_map/store/pallas_call | solution.py:440
